TPU v7x, 128 devices: a whole 4x4x4 slice. The times are simulated.
128 devices in a mesh: unit: 2 (over y_lo), pool: 64 (over z, x, y_hi, core).
Axes of the slice: x: 4, y: 4 (y_hi: 2, y_lo: 2; y = y_hi * 2 + y_lo), z: 4, core: 2. Of those that a mesh axis runs over, the one named last changes fastest.
Arguments:
- hidden_in: bfloat16 [128, 8192], P('unit', 'pool'), parts along dimension 0
- attn_gain: bfloat16 [8192], P('pool'), may hold values from 0.5 to 1.5
- w_query: bfloat16 [8192, 4096], P('pool'), may hold values from -0.0625 to 0.0625
- key_value_weight: bfloat16 [8192, 1024], P('pool'), may hold values from -0.25 to 0.25
- w_out: bfloat16 [4096, 8192], P(None, 'pool'), may hold values from -0.1875 to 0.1875
- ffn_gain: bfloat16 [8192], replicated, may hold values from 0.5 to 1.5
- w_gate: bfloat16 [8192, 16384], P(None, 'pool'), may hold values from -0.0625 to 0.0625
- w_up: bfloat16 [8192, 16384], P(None, 'pool'), may hold values from -0.0625 to 0.0625
- w_down: bfloat16 [16384, 8192], P('pool'), may hold values from -0.09375 to 0.09375
- cached_key_slots: bfloat16 [655360, 512], P(('unit', 'pool')), parts along dimension 0
- cached_value_slots: bfloat16 [655360, 512], P(('unit', 'pool')), parts along dimension 0, may hold values from -6 to 6
- lengths: int32 [128], P('unit'), parts along dimension 0, may hold values from 1024 to 5120, as said below
- home_device: int32 [128], P('unit'), parts along dimension 0, may hold values from 0 to 63, as said below
- offset: int32 [128], P('unit'), parts along dimension 0, may hold values from 0 to 4097, as said below
Outputs:
- hidden_out: bfloat16 [128, 8192], P('unit', 'pool'), parts along dimension 0
There are 2 independent parts, one for each index of `unit`. A program takes and returns all parts, laid end to end along the dimension named above; an argument that names none is the same for every part. Nothing has to cross between parts.
Inputs may be any that keep to these rules, and one draw needn't show every extreme that they name: `lengths`: A request whose device holds k requests has at most 5120 // k; one request has exactly 5120 and one exactly 1024. `home_device`: in some order the devices hold 4, 3, 2 and 2 requests, then 64 - 11 devices one each, and the other seven none. `offset`: the requests of one device occupy disjoint runs of lengths - 1 slots within its 5120 slots, in row order.
All inputs are finite; a program needn't handle non-finite values.
Results may differ from a plain program's by a relative error of at most 0.015.
Values may be sent and summed in bfloat16 or wider, within the bound.
A program may use at most 128 MiB of HBM per device.

v0:
```python
import jax
import jax.numpy as jnp
from jax import lax
from jax.sharding import PartitionSpec as P

QUERY_HEADS = 32
KEY_VALUE_HEADS = 4
HEAD_DIM = 128
MAXREQ = 4


EPSILON = 1e-05


def attend_local(
    device_query_rows, device_fresh_rows, cached_key_slots, cached_value_slots, start, length
):
    slot_count = device_query_rows.shape[0]
    group_size = QUERY_HEADS // KEY_VALUE_HEADS
    key_value_width = KEY_VALUE_HEADS * HEAD_DIM
    total_slot_count = cached_key_slots.shape[0]
    query_head_rows = device_query_rows.reshape(slot_count, KEY_VALUE_HEADS, group_size, HEAD_DIM)
    key_head_rows = cached_key_slots.reshape(total_slot_count, KEY_VALUE_HEADS, HEAD_DIM)
    value_head_rows = cached_value_slots.reshape(total_slot_count, KEY_VALUE_HEADS, HEAD_DIM)
    current_key = device_fresh_rows[:, :key_value_width].reshape(
        slot_count, KEY_VALUE_HEADS, HEAD_DIM
    )
    current_value = device_fresh_rows[:, key_value_width:].reshape(
        slot_count, KEY_VALUE_HEADS, HEAD_DIM
    )
    factor = HEAD_DIM ** (-0.5)
    scores = (
        jnp.einsum(
            "mkgd,ckd->mkgc", query_head_rows, key_head_rows, preferred_element_type=jnp.float32
        )
        * factor
    )
    slots = jnp.arange(total_slot_count, dtype=jnp.int32)
    live = (slots[None, :] >= start[:, None]) & (slots[None, :] < (start + length - 1)[:, None])
    live = live[:, None, None, :]
    scores = jnp.where(live, scores, -1e30)
    own_score = (
        jnp.einsum(
            "mkgd,mkd->mkg", query_head_rows, current_key, preferred_element_type=jnp.float32
        )
        * factor
    )
    top = jnp.maximum(jnp.max(scores, axis=-1), own_score)
    weights = jnp.where(live, jnp.exp(scores - top[..., None]), 0.0)
    own_weight = jnp.exp(own_score - top)
    total = jnp.sum(weights, axis=-1) + own_weight
    rounded = weights.astype(jnp.bfloat16)
    own_rounded = own_weight.astype(jnp.bfloat16).astype(jnp.float32)
    mixed = jnp.einsum(
        "mkgc,ckd->mkgd", rounded, value_head_rows, preferred_element_type=jnp.float32
    )
    mixed = mixed + own_rounded[..., None] * current_value.astype(jnp.float32)[:, :, None, :]
    return (
        (mixed / total[..., None]).reshape(slot_count, QUERY_HEADS * HEAD_DIM).astype(jnp.bfloat16)
    )


def local(
    hidden_in,
    attn_gain,
    w_query,
    key_value_weight,
    w_out,
    ffn_gain,
    w_gate,
    w_up,
    w_down,
    cached_key_slots,
    cached_value_slots,
    lengths,
    home_device,
    offset,
):
    rows, local_width = hidden_in.shape
    model_width = ffn_gain.shape[0]
    device = lax.axis_index("pool")
    floats = hidden_in.astype(jnp.float32)
    squares = lax.psum(jnp.sum(floats * floats, axis=1), "pool")
    factor = lax.rsqrt(squares / model_width + EPSILON)
    normed = (floats * factor[:, None] * attn_gain.astype(jnp.float32)).astype(jnp.bfloat16)
    query_part = jnp.dot(normed, w_query, preferred_element_type=jnp.float32)
    fresh_part = jnp.dot(normed, key_value_weight, preferred_element_type=jnp.float32)
    query_sum, fresh_sum = lax.psum((query_part, fresh_part), "pool")
    queries = query_sum.astype(jnp.bfloat16)
    fresh = fresh_sum.astype(jnp.bfloat16)
    row_ids = jnp.arange(rows, dtype=jnp.int32)
    same = home_device[:, None] == home_device[None, :]
    earlier = row_ids[None, :] < row_ids[:, None]
    rank = jnp.sum(same & earlier, axis=1)
    local_slots = jnp.arange(MAXREQ, dtype=jnp.int32)
    chosen = (home_device[None, :] == device) & (rank[None, :] == local_slots[:, None])
    picker = chosen.astype(jnp.bfloat16)
    device_query_rows = jnp.dot(picker, queries, preferred_element_type=jnp.float32).astype(
        jnp.bfloat16
    )
    device_fresh_rows = jnp.dot(picker, fresh, preferred_element_type=jnp.float32).astype(
        jnp.bfloat16
    )
    local_start = jnp.sum(jnp.where(chosen, offset[None, :], 0), axis=1)
    local_length = jnp.sum(jnp.where(chosen, lengths[None, :], 0), axis=1)
    attended = attend_local(
        device_query_rows,
        device_fresh_rows,
        cached_key_slots,
        cached_value_slots,
        local_start,
        local_length,
    )
    spread = jnp.einsum("mr,mc->rc", picker, attended, preferred_element_type=jnp.float32)
    attn_rows = lax.psum(spread, "pool").astype(jnp.bfloat16)
    residual = (floats + jnp.dot(attn_rows, w_out, preferred_element_type=jnp.float32)).astype(
        jnp.bfloat16
    )
    residual_floats = residual.astype(jnp.float32)
    gain_local = lax.dynamic_slice_in_dim(ffn_gain, device * local_width, local_width).astype(
        jnp.float32
    )
    ffn_squares = lax.psum(jnp.sum(residual_floats * residual_floats, axis=1), "pool")
    ffn_factor = lax.rsqrt(ffn_squares / model_width + EPSILON)
    normed_local = (residual_floats * ffn_factor[:, None] * gain_local).astype(jnp.bfloat16)
    piece = lax.all_gather(normed_local, "pool", axis=1, tiled=True)
    gate = jnp.dot(piece, w_gate, preferred_element_type=jnp.float32)
    upward = jnp.dot(piece, w_up, preferred_element_type=jnp.float32)
    inner = (jax.nn.silu(gate) * upward).astype(jnp.bfloat16)
    down = jnp.dot(inner, w_down, preferred_element_type=jnp.float32)
    shares = lax.psum_scatter(down, "pool", scatter_dimension=1, tiled=True)
    return (residual_floats + shares).astype(jnp.bfloat16)


def solution(mesh):
    return jax.shard_map(
        local,
        mesh=mesh,
        in_specs=(
            P("unit", "pool"),
            P("pool"),
            P("pool", None),
            P("pool", None),
            P(None, "pool"),
            P(),
            P(None, "pool"),
            P(None, "pool"),
            P("pool", None),
            P(("unit", "pool"), None),
            P(("unit", "pool"), None),
            P("unit"),
            P("unit"),
            P("unit"),
        ),
        out_specs=P("unit", "pool"),
        check_vma=False,
    )
```

profile of v0, /device:TPU:1, one launch (start us, length us, event | category | flops | bytes accessed | tf_op | source)
XLA Modules:
  0.0 1448.2 jit_solution(7500941168844454671)
XLA Ops:
  6.5 0.0 copy-start
  6.5 0.0 all-gather.2.cloned.1.call-start
  6.5 0.9 convert_reduce_fusion
  7.5 0.7 broadcast_compare_fusion
  8.1 0.7 convert_element_type.73
  8.8 0.8 fusion.45
  9.6 164.9 %psum.35 = f32[64]{0:T(128)S(1)} all-reduce(f32[64]{0:T(128)S(1)} %fusion.45), channel_id=1, replica_groups=mesh['unit'=2,'pool'=64] {'pool'}, use_global_device_ids=true, to_apply=%region_4.0 | all-reduce | flops 64 | bytes 512 | tf_op jit(solution)/shard_map/psum | solution.py:83
  174.5 0.8 select_reduce_fusion
  175.3 0.1 fusion.39
  175.5 1.2 fusion.55
  176.7 0.0 copy-done
  176.7 1.1 fusion.57
  177.7 334.2 %all-reduce.3 = (bf16[64,4096]{1,0:T(8,128)(2,1)S(1)}, bf16[64,1024]{1,0:T(8,128)(2,1)S(1)}) all-reduce(f32[64,4096]{1,0:T(8,128)S(1)} %fusion.57, f32[64,1024]{1,0:T(8,128)S(1)} %fusion.55), channel_id=1, replica_groups=mesh['unit'=2,'pool'=64] {'pool'}, use_global_device_ids=true, to_apply=%region_5.6 | all-reduce | flops 327680 | bytes 1966080 | tf_op jit(solution)/shard_map/psum | solution.py:88
  511.9 0.2 fusion.22
  512.1 0.1 convolution_convert_fusion.1
  512.3 8.3 reshape.78
  520.6 0.1 fusion.66
  520.7 4.4 fusion.65
  525.2 0.0 copy-start.1
  525.2 1.5 copy-done.1
  526.7 0.7 fusion.5
  527.4 8.3 reshape.80
  535.7 0.0 copy-start.3
  535.7 4.4 fusion.31
  540.2 0.3 fusion.48
  540.5 331.8 %all-reduce.4 = bf16[64,4096]{1,0:T(8,128)(2,1)S(1)} all-reduce(f32[64,4096]{1,0:T(8,128)S(1)} %fusion.48), channel_id=1, replica_groups=mesh['unit'=2,'pool'=64] {'pool'}, use_global_device_ids=true, to_apply=%region_9.10 | all-reduce | flops 262144 | bytes 1572864 | tf_op jit(solution)/shard_map/psum | solution.py:115
  872.4 0.0 copy-done.3
  872.4 1.6 multiply_reduce_fusion
  874.0 170.0 %psum.39 = f32[64]{0:T(128)S(1)} all-reduce(f32[64]{0:T(128)S(1)} %get-tuple-element.16), channel_id=1, replica_groups=mesh['unit'=2,'pool'=64] {'pool'}, use_global_device_ids=true, to_apply=%region_11.12 | all-reduce | flops 64 | bytes 512 | tf_op jit(solution)/shard_map/psum | solution.py:123
  1044.0 0.8 dynamic-slice_convert_fusion
  1044.8 0.7 multiply_convert_fusion
  1045.5 0.0 all-gather.2.cloned.1.call-update
  1045.5 0.0 reduce-scatter.2.cloned.1.call-start
  1045.5 56.8 %all-gather.2.cloned.1.call-done = bf16[64,8192]{1,0:T(8,128)(2,1)} async-done(((bf16[64,128]{1,0:T(8,128)(2,1)}), bf16[64,8192]{1,0:T(8,128)(2,1)}) %all-gather.2.cloned.1.call-update) | async-done | bytes 1048592 | tf_op jit(solution)/shard_map/all_gather | solution.py:126
  1102.3 0.0 copy-start.2
  1102.3 3.4 fusion.67
  1105.7 0.0 copy-done.2
  1105.7 7.4 fusion.23
  1113.1 0.0 reduce-scatter.2.cloned.1.call-update
  1113.1 326.9 %reduce-scatter.2.cloned.1.call-done = f32[64,128]{1,0:T(8,128)} async-done(((f32[64,8192]{1,0:T(8,128)}), f32[64,128]{1,0:T(8,128)}) %reduce-scatter.2.cloned.1.call-update) | async-done | bytes 32784 | tf_op jit(solution)/shard_map/reduce_scatter | solution.py:131
  1440.0 1.4 add_convert_fusion
  (8 shorter events, 0.1 us)
Async XLA Ops:
  6.5 170.1 %copy-start = (bf16[128,4096]{1,0:T(8,128)(2,1)S(1)}, bf16[128,4096]{1,0:T(8,128)(2,1)}, u32[]{:S(2)}) copy-start(bf16[128,4096]{1,0:T(8,128)(2,1)} %param.16) | copy-start | bytes 3145732
  6.5 1095.7 %all-gather.2.cloned.1.call-start = ((), (), s32[]{:S(2)}) async-start(), calls=%async_computation.1 | async-start | bytes 1064960 | tf_op jit(solution)/shard_map/all_gather | solution.py:126
  525.2 1.5 copy-start.1
  535.7 336.6 %copy-start.3 = (bf16[64,128]{1,0:T(8,128)(2,1)S(1)}, bf16[64,128]{1,0:T(8,128)(2,1)}, u32[]{:S(2)}) copy-start(bf16[64,128]{1,0:T(8,128)(2,1)} %param.14) | copy-start | bytes 49156
  1045.5 394.5 %reduce-scatter.2.cloned.1.call-start = ((), (), s32[]{:S(2)}) async-start(), calls=%async_computation.2 | async-start | bytes 2129920 | tf_op jit(solution)/shard_map/reduce_scatter | solution.py:131
  1102.3 3.4 copy-start.2
Sparse Core Ops, SparseCore 0:
  1045.6 56.6 all-gather.1
  1113.2 326.7 reduce-scatter.1
where the time goes:
time: 1460 us; the launch traced here: 1450 us
  blocking collectives  1000 us (68%)
  waiting for transfers between devices  384 us (26%)
  matrix products  24.4 us (2%)
  local copies, waits for them, and re-layouts  18.2 us (1%)
    psum x1, blocking collectives, local(): query_sum, fresh_sum = lax.psum((query_part, fresh_part), 'pool')  334 us
    psum x1, blocking collectives, local(): attn_rows = lax.psum(spread, 'pool').astype(jnp.bfloat16)  332 us
    reduce_scatter x1, waiting for transfers between devices, local(): shares = lax.psum_scatter(down, 'pool', scatter_dimension=1, tiled=True)  327 us
    psum x1, blocking collectives, local(): lax.psum(jnp.sum(residual_floats * residual_floats, axis=1), 'pool')  170 us
    psum x1, blocking collectives, local(): squares = lax.psum(jnp.sum(floats * floats, axis=1), 'pool')  165 us
    all_gather x1, waiting for transfers between devices, local(): piece = lax.all_gather(normed_local, 'pool', axis=1, tiled=True)  56.8 us
  transfers between devices with their start and end apart: 2, of which 2 were waited for; matrix products, arithmetic and copies ran while one was open for 0% of the time, Pallas kernels for 0%

commit v1 on v0

v1 whole, which is shorter than its diff:
```python
import jax
import jax.numpy as jnp
from jax import lax
from jax.experimental import pallas as pl
from jax.experimental.pallas import tpu as pltpu
from jax.sharding import PartitionSpec as P

MESH = pl.DeviceIdType.MESH
F32 = jnp.float32
BF16 = jnp.bfloat16
EPSILON = 1e-05
MODEL = 8192
SLOTS = 5120
CHUNK = 512
SHIFTS = (2, 1, 3, 0)
EXTRA = 7


def dot(a, b):
    return jnp.dot(a, b, preferred_element_type=F32)


def iota(shape, axis):
    return lax.broadcasted_iota(jnp.int32, shape, axis)


def kernel(
    hidden_ref,
    gain_ref,
    ffn_gain_ref,
    lengths_ref,
    home_ref,
    offset_ref,
    wq_hbm,
    wkv_hbm,
    wout_hbm,
    wgate_hbm,
    wup_hbm,
    wdown_hbm,
    keys_hbm,
    values_hbm,
    out_ref,
    wq,
    wkv,
    wout,
    wgate,
    wup,
    wdown,
    keys,
    values,
    blk,
    ext,
    sib_out,
    sib_in,
    rs_out,
    rs_in,
    qe_buf,
    qe,
    scores,
    att_buf,
    xo_out,
    xo_in,
    xr_out,
    xr_in,
    xa_buf,
    spread,
    lhs,
    res_buf,
    lhs_ffn,
    stage,
    dsib_out,
    dsib_in,
    drs_out,
    drs_in,
    load_sem,
    sib_send,
    sib_recv,
    rs_send,
    rs_recv,
    ag_send,
    ag_recv,
    fwd_send,
    fwd_recv,
    dsib_send,
    dsib_recv,
):
    me = lax.axis_index("pool")
    chip = lax.div(me, 2)
    core = lax.rem(me, 2)
    z = lax.div(chip, 8)
    x = lax.rem(lax.div(chip, 2), 4)
    y = lax.rem(chip, 2)
    sibling = chip * 2 + (1 - core)
    my_slot = core * 32 + chip

    def target(a, k):
        b = 3 - lax.div(k, 2)
        e = 1 - lax.rem(k, 2)
        return lax.rem(z + a, 4) * 8 + lax.rem(x + b, 4) * 2 + lax.rem(y + e, 2)

    def each_chip(body):
        for a in SHIFTS:

            def step(k, carry, a=a):
                body(a, target(a, k))
                return carry

            lax.fori_loop(0, 8 if a else 7, step, 0)

    def remote(src, dst, send, recv, chip_to):
        return pltpu.make_async_remote_copy(
            src_ref=src,
            dst_ref=dst,
            send_sem=send,
            recv_sem=recv,
            device_id={"pool": chip_to * 2 + core},
            device_id_type=MESH,
        )

    def to_sibling(src, dst, send, recv):
        return pltpu.make_async_remote_copy(
            src_ref=src,
            dst_ref=dst,
            send_sem=send,
            recv_sem=recv,
            device_id={"pool": sibling},
            device_id_type=MESH,
        )

    barrier = pltpu.get_barrier_semaphore()
    each_chip(
        lambda a, c: pl.semaphore_signal(
            barrier, inc=1, device_id={"pool": c * 2 + core}, device_id_type=MESH
        )
    )
    pl.semaphore_signal(barrier, inc=1, device_id={"pool": sibling}, device_id_type=MESH)

    loads = [
        pltpu.make_async_copy(src, dst, load_sem.at[i])
        for i, (src, dst) in enumerate(
            [
                (wq_hbm, wq),
                (wkv_hbm, wkv),
                (keys_hbm, keys),
                (values_hbm, values),
                (wout_hbm, wout),
                (wgate_hbm, wgate),
                (wup_hbm, wup),
                (wdown_hbm, wdown),
            ]
        )
    ]
    for load in loads:
        load.start()

    home_row = jnp.broadcast_to(home_ref[...].astype(F32), (64, 64))
    down_i = iota((64, 64), 0)
    along_i = iota((64, 64), 1)
    eye = down_i == along_i

    def column(row):
        return jnp.sum(jnp.where(eye, row, 0.0), axis=1, keepdims=True)

    home_col = column(home_row)
    same = jnp.where(home_col == home_row, 1.0, 0.0)
    rank_row = jnp.sum(jnp.where(down_i < along_i, same, 0.0), axis=0, keepdims=True)
    rank_col = jnp.sum(jnp.where(along_i < down_i, same, 0.0), axis=1, keepdims=True)
    extra_col = jnp.where(rank_col > 0.0, 1.0, 0.0)
    extra_row = jnp.where(rank_row > 0.0, 1.0, 0.0)
    order_row = jnp.sum(jnp.where(down_i < along_i, extra_col, 0.0), axis=0, keepdims=True)
    order_col = jnp.sum(jnp.where(along_i < down_i, extra_row, 0.0), axis=1, keepdims=True)
    half_row = jnp.floor(home_row[:1] * 0.5)
    half_col = jnp.floor(home_col * 0.5)
    slot_row = jnp.where(
        rank_row == 0.0, (home_row[:1] - 2.0 * half_row) * 32.0 + half_row, 64.0 + order_row
    )
    slot_col = jnp.where(
        rank_col == 0.0, (home_col - 2.0 * half_col) * 32.0 + half_col, 64.0 + order_col
    )
    to_slots = jnp.where(slot_row == iota((72, 64), 0).astype(F32), 1.0, 0.0).astype(BF16)
    from_slots = jnp.where(slot_col == iota((64, 72), 1).astype(F32), 1.0, 0.0).astype(BF16)
    here_row = home_row[:1] == me.astype(F32)
    here_col = home_col == me.astype(F32)
    lane = iota((1, 128), 1)
    lane_request = lax.div(lane, 32)
    offset_row = offset_ref[...].astype(F32)
    past_row = lengths_ref[...].astype(F32) - 1.0
    start = jnp.zeros((1, 128), F32)
    stop = jnp.zeros((1, 128), F32)
    for m in range(4):
        chosen = here_row & (rank_row == float(m))
        begin = jnp.sum(jnp.where(chosen, offset_row, 0.0), axis=1, keepdims=True)
        end = begin + jnp.sum(jnp.where(chosen, past_row, 0.0), axis=1, keepdims=True)
        start = jnp.where(lane_request == m, begin, start)
        stop = jnp.where(lane_request == m, end, stop)
    start = start.astype(jnp.int32)
    stop = stop.astype(jnp.int32)
    pick_col, pick_row = [], []
    order_is = (order_row == iota((8, 64), 0).astype(F32)) & (extra_row > 0.0)
    lane64 = lax.rem(iota((64, 128), 1), 64).astype(F32)
    order_at = (order_col == lane64) & (extra_col > 0.0)
    for m in range(1, 4):
        mine = jnp.where(here_row & (rank_row == float(m)), 1.0, 0.0)
        pick_col.append(jnp.sum(jnp.where(order_is, mine, 0.0), axis=1, keepdims=True))
        mine = jnp.where(here_col & (rank_col == float(m)), 1.0, 0.0)
        pick_row.append(jnp.sum(jnp.where(order_at, mine, 0.0), axis=0, keepdims=True))

    rows = dot(to_slots, hidden_ref[...])
    squares = jnp.sum(rows * rows, axis=1, keepdims=True)
    scaled = (rows * gain_ref[...].astype(F32)).astype(BF16)
    loads[0].wait()
    loads[1].wait()
    for n in range(10):
        weight = wq[:, n * 512 : (n + 1) * 512] if n < 8 else wkv[:, (n - 8) * 512 : (n - 7) * 512]
        part = dot(scaled, weight)
        for t in range(4):
            j = 4 * n + t
            tile = part[:, t * 128 : (t + 1) * 128]
            blk[pl.ds(j, 64, stride=48), :] = tile[:64]
            ext[pl.ds(j, 8, stride=40), :] = tile[64:]
    for e in range(8):
        for r in range(5):
            blk[pl.ds(8 * e * 48 + 40 + r, 8, stride=48), :] = ext[pl.ds(e * 40 + r * 8, 8), :]

    def high_low(value, low):
        high = value.astype(BF16).astype(F32)
        return jnp.where(low, value - high, high)

    wide = jnp.broadcast_to(squares, (72, 128))
    blk[pl.ds(45, 64, stride=48), :] = high_low(wide[:64], iota((64, 128), 1) >= 64)
    extra_squares = jnp.where(lax.rem(iota((8, 128), 1), 64) == iota((8, 128), 0), wide[64:], 0.0)
    extra_squares = jnp.sum(extra_squares, axis=0, keepdims=True)
    blk[pl.ds(46, 64, stride=48), :] = jnp.broadcast_to(
        high_low(extra_squares, lane >= 64), (64, 128)
    )
    blk[pl.ds(47, 64, stride=48), :] = jnp.zeros((64, 128), F32)

    def block(slot):
        return blk[pl.ds(pl.multiple_of(slot * 48, 16), 48), :]

    def pack_sibling(k, carry):
        sib_out[k] = block((1 - core) * 32 + k).astype(BF16)
        return carry

    lax.fori_loop(0, 32, pack_sibling, 0)
    pl.semaphore_wait(barrier, 32)
    exchange = to_sibling(sib_out, sib_in, sib_send.at[0], sib_recv.at[0])
    exchange.start()
    exchange.wait()

    def pack(k, carry):
        rs_out[k] = (block(core * 32 + k) + sib_in[k].astype(F32)).astype(BF16)
        return carry

    lax.fori_loop(0, 32, pack, 0)
    each_chip(
        lambda a, c: remote(rs_out.at[c], rs_in.at[chip], rs_send.at[0], rs_recv.at[0], c).start()
    )
    rs_in[chip] = rs_out[chip]
    part31 = pl.ds(0, 31)
    done = remote(rs_out.at[part31], rs_in.at[part31], rs_send.at[0], rs_recv.at[0], chip)
    done.wait_recv()

    def add(k, total):
        return total + rs_in[k].astype(F32)

    summed = lax.fori_loop(0, 32, add, jnp.zeros((48, 128), F32))
    done.wait_send()

    def gather_start(buf, p):
        each_chip(
            lambda a, c: remote(
                buf.at[my_slot], buf.at[my_slot], ag_send.at[p], ag_recv.at[p * 4 + a], c
            ).start()
        )

    def gather_forward(buf, p):
        sends = []
        for a in SHIFTS:
            some = buf.at[pl.ds(0, 8 if a else 7)]
            remote(some, some, ag_send.at[p], ag_recv.at[p * 4 + a], chip).wait_recv()
            group = buf.at[pl.ds(core * 32 + lax.rem(z + 4 - a, 4) * 8, 8)]
            send = to_sibling(group, group, fwd_send.at[p * 4 + a], fwd_recv.at[p * 4 + a])
            send.start()
            sends.append(send)
        return sends

    def gather_end(buf, p, sends):
        for send in sends:
            send.wait()
        some = buf.at[pl.ds(0, 31)]
        remote(some, some, ag_send.at[p], ag_recv.at[p * 4], chip).wait_send()

    qe_buf[my_slot] = summed[40:48]
    gather_start(qe_buf, 0)
    sends = gather_forward(qe_buf, 0)
    gather_end(qe_buf, 0, sends)

    own_squares = jnp.sum(summed[45:46], axis=1, keepdims=True) * (1.0 / 64.0)
    requests = [summed[:40] * lax.rsqrt(own_squares * (1.0 / MODEL) + EPSILON)]
    for e in range(EXTRA):
        for r in range(5):
            piece = qe_buf[pl.ds(8 * e, 8), r, :]
            qe[e, pl.ds(8 * r, 8), :] = piece
    for m in range(3):
        total = jnp.zeros((40, 128), F32)
        for e in range(EXTRA):
            total = total + pick_col[m][e : e + 1] * qe[e]
        sq = jnp.sum(pick_row[m] * summed[46:47], axis=1, keepdims=True)
        requests.append(total * lax.rsqrt(sq * (1.0 / MODEL) + EPSILON))
    query = jnp.concatenate([r[:32] for r in requests], axis=0).astype(BF16).astype(F32)
    new_keys = jnp.concatenate([r[32:36] for r in requests], axis=0).astype(BF16)
    new_values = jnp.concatenate([r[36:40] for r in requests], axis=0).astype(BF16)
    query_t = query.T
    lane_head = lax.rem(lax.div(iota((128, 128), 1), 8), 4)
    spread_query = jnp.concatenate(
        [jnp.where(lane_head == k, query_t, 0.0) for k in range(4)], axis=0
    ).astype(BF16)
    scale = 128.0**-0.5
    own = dot(new_keys, query_t.astype(BF16)) * scale
    own = jnp.sum(
        jnp.where(lax.div(iota((16, 128), 1), 8) == iota((16, 128), 0), own, 0.0),
        axis=0,
        keepdims=True,
    )

    loads[2].wait()

    def score(i, best):
        at = pl.ds(pl.multiple_of(i * CHUNK, CHUNK), CHUNK)
        s = dot(keys[at, :], spread_query) * scale
        slot = iota((CHUNK, 128), 0) + i * CHUNK
        s = jnp.where((slot >= start) & (slot < stop), s, -jnp.inf)
        scores[at, :] = s
        return jnp.maximum(best, jnp.max(s.reshape(CHUNK // 8, 8, 128), axis=0))

    best = lax.fori_loop(0, SLOTS // CHUNK, score, jnp.full((8, 128), -jnp.inf, F32))
    top = jnp.maximum(jnp.max(best, axis=0, keepdims=True), own)
    loads[3].wait()

    def mix(i, carry):
        total, mixed = carry
        at = pl.ds(pl.multiple_of(i * CHUNK, CHUNK), CHUNK)
        w = jnp.exp(scores[at, :] - top)
        total = total + jnp.sum(w.reshape(CHUNK // 8, 8, 128), axis=0)
        mixed = mixed + lax.dot_general(
            w.astype(BF16), values[at, :], (((0,), (0,)), ((), ())), preferred_element_type=F32
        )
        return total, mixed

    total, mixed = lax.fori_loop(
        0, SLOTS // CHUNK, mix, (jnp.zeros((8, 128), F32), jnp.zeros((128, 512), F32))
    )
    own_weight = jnp.exp(own - top)
    total = jnp.sum(total, axis=0, keepdims=True) + own_weight
    eye128 = iota((128, 128), 0) == iota((128, 128), 1)
    total_col = jnp.sum(jnp.where(eye128, total, 0.0), axis=1, keepdims=True)
    own_col = jnp.sum(jnp.where(eye128, own_weight, 0.0), axis=1, keepdims=True)
    row_head = lax.rem(lax.div(iota((128, 128), 0), 8), 4)
    att = jnp.zeros((128, 128), F32)
    for k in range(4):
        att = jnp.where(row_head == k, mixed[:, k * 128 : (k + 1) * 128], att)
    own_spread = jnp.where(lax.div(iota((128, 16), 0), 8) == iota((128, 16), 1), own_col, 0.0)
    att = (att + dot(own_spread.astype(BF16), new_values)) / total_col

    att_buf[my_slot] = att[:32].astype(BF16)
    gather_start(att_buf, 1)
    for e in range(EXTRA):
        piece = jnp.zeros((32, 128), F32)
        for m in range(3):
            piece = piece + pick_col[m][e : e + 1] * att[32 * (m + 1) : 32 * (m + 2)]
        xo_out[2 * e] = piece[:16].astype(BF16)
        xo_out[2 * e + 1] = piece[16:].astype(BF16)
    exchange = to_sibling(
        xo_out.at[pl.ds((1 - core) * 7, 7)], xo_in, sib_send.at[1], sib_recv.at[1]
    )
    exchange.start()
    exchange.wait()

    def reducer(j):
        return 5 * j + core

    def reduce_send(j, carry):
        xr_out[j] = (xo_out[core * 7 + j].astype(F32) + xo_in[j].astype(F32)).astype(BF16)

        @pl.when(reducer(j) == chip)
        def _():
            xr_in[chip] = xr_out[j]

        @pl.when(reducer(j) != chip)
        def _():
            remote(
                xr_out.at[j], xr_in.at[chip], rs_send.at[1], rs_recv.at[1], reducer(j)
            ).start()

        return carry

    lax.fori_loop(0, 7, reduce_send, 0)
    is_reducer = lax.rem(chip + 5 - core, 5) == 0
    my_chunk = lax.div(chip - core, 5)

    def many(ref, n, send, recv):
        some = ref.at[pl.ds(0, n)]
        return remote(some, some, send, recv, chip)

    @pl.when(is_reducer)
    def _():
        many(xr_in, 31, rs_send.at[1], rs_recv.at[1]).wait_recv()
        xa_buf[core * 7 + my_chunk] = lax.fori_loop(
            0, 32, lambda k, t: t + xr_in[k].astype(F32), jnp.zeros((16, 128), F32)
        ).astype(BF16)
        mine = xa_buf.at[core * 7 + my_chunk]
        each_chip(lambda a, c: remote(mine, mine, rs_send.at[2], rs_recv.at[2], c).start())
        many(xr_out, 6, rs_send.at[1], rs_recv.at[1]).wait_send()
        many(xa_buf, 6, rs_send.at[2], rs_recv.at[2]).wait_recv()

    @pl.when(jnp.logical_not(is_reducer))
    def _():
        many(xr_out, 7, rs_send.at[1], rs_recv.at[1]).wait_send()
        many(xa_buf, 7, rs_send.at[2], rs_recv.at[2]).wait_recv()

    half = xa_buf.at[pl.ds(core * 7, 7)]
    exchange = to_sibling(half, half, sib_send.at[2], sib_recv.at[2])
    exchange.start()
    sends = gather_forward(att_buf, 1)
    gather_end(att_buf, 1, sends)
    exchange.wait()

    @pl.when(is_reducer)
    def _():
        many(xr_in, 31, rs_send.at[2], rs_recv.at[2]).wait_send()

    def widen(s, carry):
        spread[pl.ds(pl.multiple_of(s * 32, 32), 32), :] = att_buf[s].astype(F32)
        return carry

    lax.fori_loop(0, 64, widen, 0)
    for q in range(14):
        spread[pl.ds(2048 + 16 * q, 16), :] = xa_buf[q].astype(F32)
    spread[pl.ds(2048 + 224, 32), :] = jnp.zeros((32, 128), F32)
    for h in range(32):
        lhs[:, h * 128 : (h + 1) * 128] = spread[pl.ds(h, 72, stride=32), :].astype(BF16)
    loads[4].wait()
    projected = dot(lhs[...], wout[...])
    moved = jnp.zeros((64, 128), F32)
    for _ in range(3):
        piece = projected.astype(BF16)
        moved = moved + dot(from_slots, piece)
        projected = projected - piece.astype(F32)
    residual = (hidden_ref[...].astype(F32) + moved).astype(BF16)

    res_buf[my_slot] = residual
    gather_start(res_buf, 2)
    sends = gather_forward(res_buf, 2)
    gather_end(res_buf, 2, sends)

    def scale_ffn(p, squares):
        value = res_buf[lax.rem(p, 2) * 32 + lax.div(p, 2)].astype(F32)
        gain = ffn_gain_ref[pl.ds(p, 1), :]
        lhs_ffn[:, pl.ds(pl.multiple_of(p * 128, 128), 128)] = (value * gain).astype(BF16)
        return squares + value * value

    squares = lax.fori_loop(0, 64, scale_ffn, jnp.zeros((64, 128), F32))
    factor = lax.rsqrt(jnp.sum(squares, axis=1, keepdims=True) * (1.0 / MODEL) + EPSILON)
    loads[5].wait()
    loads[6].wait()

    def hidden_units(i, carry):
        gate, up = carry
        at = pl.ds(pl.multiple_of(i * 1024, 1024), 1024)
        some = lhs_ffn[:, at]
        return gate + dot(some, wgate[at, :]), up + dot(some, wup[at, :])

    zero = jnp.zeros((64, 256), F32)
    gate, up = lax.fori_loop(0, 8, hidden_units, (zero, zero))
    gate = gate * factor
    inner = (gate / (1.0 + jnp.exp(-gate)) * (up * factor)).astype(BF16)

    loads[7].wait()
    exchanges = []
    for i, a in enumerate(SHIFTS):
        first = lax.rem(z + a, 4)
        for n in range(4):
            at = pl.multiple_of(first * 2048 + n * 512, 512)
            part = dot(inner, wdown[:, pl.ds(at, 512)])
            for t in range(4):
                stage[16 * i + 4 * n + t] = part[:, t * 128 : (t + 1) * 128]

        def pack_down(k, carry, i=i):
            dsib_out[8 * i + k] = stage[16 * i + 2 * k + 1 - core].astype(BF16)
            return carry

        lax.fori_loop(0, 8, pack_down, 0)
        group = pl.ds(8 * i, 8)
        exchange = to_sibling(
            dsib_out.at[group], dsib_in.at[group], dsib_send.at[i], dsib_recv.at[i]
        )
        exchange.start()
        exchanges.append(exchange)
    for i, a in enumerate(SHIFTS):
        exchanges[i].wait_recv()
        first = lax.rem(z + a, 4) * 8

        def send_down(k, carry, a=a, i=i, first=first):
            c = target(a, k)
            n = 8 * i + c - first
            total = stage[16 * i + 2 * (c - first) + core] + dsib_in[n].astype(F32)
            drs_out[n] = total.astype(BF16)
            remote(drs_out.at[n], drs_in.at[chip], rs_send.at[3], rs_recv.at[3], c).start()
            return carry

        lax.fori_loop(0, 8 if a else 7, send_down, 0)
    k = chip - z * 8
    drs_in[chip] = (stage[48 + 2 * k + core] + dsib_in[24 + k].astype(F32)).astype(BF16)
    done = many(drs_in, 31, rs_send.at[3], rs_recv.at[3])
    done.wait_recv()
    shares = lax.fori_loop(
        0, 32, lambda k, t: t + drs_in[k].astype(F32), jnp.zeros((64, 128), F32)
    )
    out_ref[...] = (residual.astype(F32) + shares).astype(BF16)
    done.wait_send()
    for exchange in exchanges:
        exchange.wait_send()


def local(
    hidden_in,
    attn_gain,
    w_query,
    key_value_weight,
    w_out,
    ffn_gain,
    w_gate,
    w_up,
    w_down,
    cached_key_slots,
    cached_value_slots,
    lengths,
    home_device,
    offset,
):
    vmem = pl.BlockSpec(memory_space=pltpu.VMEM)
    hbm = pl.BlockSpec(memory_space=pl.ANY)
    V = pltpu.VMEM
    dma = pltpu.SemaphoreType.DMA
    return pl.pallas_call(
        kernel,
        out_shape=jax.ShapeDtypeStruct((64, 128), BF16),
        in_specs=[vmem] * 6 + [hbm] * 8,
        out_specs=vmem,
        scratch_shapes=[
            V((128, 4096), BF16),
            V((128, 1024), BF16),
            V((4096, 128), BF16),
            V((8192, 256), BF16),
            V((8192, 256), BF16),
            V((256, 8192), BF16),
            V((SLOTS, 512), BF16),
            V((SLOTS, 512), BF16),
            V((64 * 48, 128), F32),
            V((320, 128), F32),
            V((32, 48, 128), BF16),
            V((32, 48, 128), BF16),
            V((32, 48, 128), BF16),
            V((32, 48, 128), BF16),
            V((64, 8, 128), F32),
            V((7, 40, 128), F32),
            V((SLOTS, 128), F32),
            V((64, 32, 128), BF16),
            V((14, 16, 128), BF16),
            V((7, 16, 128), BF16),
            V((7, 16, 128), BF16),
            V((32, 16, 128), BF16),
            V((14, 16, 128), BF16),
            V((72 * 32, 128), F32),
            V((72, 4096), BF16),
            V((64, 64, 128), BF16),
            V((64, 8192), BF16),
            V((64, 64, 128), F32),
            V((32, 64, 128), BF16),
            V((32, 64, 128), BF16),
            V((32, 64, 128), BF16),
            V((32, 64, 128), BF16),
            dma((8,)),
            dma((3,)),
            dma((3,)),
            dma((4,)),
            dma((4,)),
            dma((3,)),
            dma((12,)),
            dma((12,)),
            dma((12,)),
            dma((4,)),
            dma((4,)),
        ],
        compiler_params=pltpu.CompilerParams(
            collective_id=0, has_side_effects=True, vmem_limit_bytes=60 << 20
        ),
    )(
        hidden_in,
        attn_gain.reshape(1, 128),
        ffn_gain.reshape(64, 128).astype(F32),
        lengths.reshape(1, 64),
        home_device.reshape(1, 64),
        offset.reshape(1, 64),
        w_query,
        key_value_weight,
        w_out,
        w_gate,
        w_up,
        w_down,
        cached_key_slots,
        cached_value_slots,
    )


def solution(mesh):
    return jax.shard_map(
        local,
        mesh=mesh,
        in_specs=(
            P("unit", "pool"),
            P("pool"),
            P("pool", None),
            P("pool", None),
            P(None, "pool"),
            P(),
            P(None, "pool"),
            P(None, "pool"),
            P("pool", None),
            P(("unit", "pool"), None),
            P(("unit", "pool"), None),
            P("unit"),
            P("unit"),
            P("unit"),
        ),
        out_specs=P("unit", "pool"),
        check_vma=False,
    )
```

time: 1460 us -> 79.8 us (0.05)
  blocking collectives: 1000 us -> 0 us
  waiting for transfers between devices: 384 us -> 0 us
  Pallas kernels: 0 us -> 76.9 us
  matrix products: 24.4 us -> 0 us
  local copies, waits for them, and re-layouts: 18.2 us -> 1.32 us
    psum x4 -> x0, blocking collectives: 1000 us -> none  [the longest x1 334 us: local(): query_sum, fresh_sum = lax.psum((query_part, fresh_part), 'pool')]
    reduce_scatter x1 -> x0, waiting for transfers between devices: 327 us -> none  [local(): shares = lax.psum_scatter(down, 'pool', scatter_dimension=1, tiled=True)]
    pallas_call x0 -> x1, Pallas kernels: none -> 76.9 us  [local(): pl.pallas_call(kernel, out_shape=jax.ShapeDtypeStruct((64, 128), BF16), i...]
    all_gather x1 -> x0, waiting for transfers between devices: 56.8 us -> none  [local(): piece = lax.all_gather(normed_local, 'pool', axis=1, tiled=True)]
    dot_general x11 -> x0, matrix products: 24.4 us -> none  [the longest x1 7.41 us: local(): down = jnp.dot(inner, w_down, preferred_element_type=jnp.float32)]
    reshape x3 -> x0, local copies, waits for them, and re-layouts: 16.7 us -> none  [the longest x1 8.34 us: attend_local(): cached_value_slots.reshape(total_slot_count, KEY_VALUE_HEADS, HEAD_DIM)]
  transfers between devices with their start and end apart: 2 -> 0, of which waited for: 2 -> 0; matrix products, arithmetic and copies ran while one was open for 0% -> 0% of each run, Pallas kernels for 0% -> 0%
where the time goes in v1:
time: 79.8 us; the launch traced here: 79.6 us
  Pallas kernels  76.9 us (96%)
  other arithmetic  1.32 us (2%)
  local copies, waits for them, and re-layouts  1.32 us (2%)
    pallas_call x1, Pallas kernels, local(): pl.pallas_call(kernel, out_shape=jax.ShapeDtypeStruct((64, 128), BF16), i...  76.9 us

profile of v1, /device:TPU:1, one launch (start us, length us, event | category | flops | bytes accessed | tf_op | source)
XLA Modules:
  0.0 79.6 jit_solution(3348110251942065681)
XLA Ops:
  0.0 1.3 %bitcast_convert_fusion.ffn_gain_ref = f32[64,128]{1,0:T(8,128)} fusion(bf16[8192]{0:T(1024)(128)(2,1)} %param.19), kind=kLoop, calls=%fused_computation | loop fusion | flops 8192 | bytes 49152 | tf_op jit(solution)/shard_map/convert_element_type | solution.py:602
  1.3 76.9 %shard_map.136 = bf16[64,128]{1,0:T(8,128)(2,1)} custom-call(bf16[64,128]{1,0:T(8,128)(2,1)} %hidden_ref.1, bf16[1,128]{1,0:T(2,128)(2,1)} %bitcast.7, f32[64,128]{1,0:T(8,128)} %bitcast_convert_fusion.ffn_gain_ref, s32[1,64]{1,0:T(1,128)} %bitcast.8, s32[1,64]{1,0:T(1,128)} %bitcast.9, s32[1,64]{1,0:T(1,128)} %bitcast.10, bf16[128,4096]{1,0:T(8,128)(2,1)} %wq_hbm.1, ...), custom_call_target="tpu_custom_call" | custom-call | tf_op jit(solution)/shard_map/pallas_call | solution.py:546
  78.2 1.3 %copy.16 = bf16[64,128]{1,0:T(8,128)(2,1)} copy(bf16[64,128]{1,0:T(8,128)(2,1)} %shard_map.136) | data formatting | bytes 32768

commit v2 on v1

--- a/solution.py
+++ b/solution.py
@@ -54,19 +54,18 @@
     sib_in,
     rs_out,
     rs_in,
-    qe_buf,
-    qe,
+    xq_out,
+    xq_in,
+    xq_buf,
     scores,
     att_buf,
-    xo_out,
-    xo_in,
-    xr_out,
-    xr_in,
+    xa_out,
+    xa_in,
     xa_buf,
     spread,
+    spread_extra,
     lhs,
     res_buf,
-    lhs_ffn,
     stage,
     dsib_out,
     dsib_in,
@@ -75,6 +74,8 @@
     load_sem,
     sib_send,
     sib_recv,
+    ring_send,
+    ring_recv,
     rs_send,
     rs_recv,
     ag_send,
@@ -127,6 +128,12 @@
             device_id_type=MESH,
         )
 
+    member = x * 2 + core
+
+    def ring_member(i):
+        g = lax.rem(member + i, 8)
+        return g, (z * 8 + lax.div(g, 2) * 2 + y) * 2 + lax.rem(g, 2)
+
     barrier = pltpu.get_barrier_semaphore()
     each_chip(
         lambda a, c: pl.semaphore_signal(
@@ -134,6 +141,9 @@
         )
     )
     pl.semaphore_signal(barrier, inc=1, device_id={"pool": sibling}, device_id_type=MESH)
+    for i in range(1, 4):
+        other = (z * 8 + lax.rem(x + i, 4) * 2 + y) * 2 + 1 - core
+        pl.semaphore_signal(barrier, inc=1, device_id={"pool": other}, device_id_type=MESH)
 
     loads = [
         pltpu.make_async_copy(src, dst, load_sem.at[i])
@@ -150,8 +160,8 @@
             ]
         )
     ]
-    for load in loads:
-        load.start()
+    loads[0].start()
+    loads[1].start()
 
     home_row = jnp.broadcast_to(home_ref[...].astype(F32), (64, 64))
     down_i = iota((64, 64), 0)
@@ -178,7 +188,7 @@
         rank_col == 0.0, (home_col - 2.0 * half_col) * 32.0 + half_col, 64.0 + order_col
     )
     to_slots = jnp.where(slot_row == iota((72, 64), 0).astype(F32), 1.0, 0.0).astype(BF16)
-    from_slots = jnp.where(slot_col == iota((64, 72), 1).astype(F32), 1.0, 0.0).astype(BF16)
+    from_slots = jnp.where(slot_col == iota((64, 80), 1).astype(F32), 1.0, 0.0).astype(BF16)
     here_row = home_row[:1] == me.astype(F32)
     here_col = home_col == me.astype(F32)
     lane = iota((1, 128), 1)
@@ -195,21 +205,39 @@
         stop = jnp.where(lane_request == m, end, stop)
     start = start.astype(jnp.int32)
     stop = stop.astype(jnp.int32)
-    pick_col, pick_row = [], []
-    order_is = (order_row == iota((8, 64), 0).astype(F32)) & (extra_row > 0.0)
-    lane64 = lax.rem(iota((64, 128), 1), 64).astype(F32)
-    order_at = (order_col == lane64) & (extra_col > 0.0)
+    def floor_div(value, n):
+        return jnp.floor((value + 0.5) * (1.0 / n))
+
+    chunk_lane = iota((1, 384), 1).astype(F32)
+    chunk_of = floor_div(chunk_lane, 48)
+    chunk_row = chunk_lane - 48.0 * chunk_of
+    extra_of = floor_div(chunk_row, 5)
+    tile_of = 5.0 * chunk_of + chunk_row - 5.0 * extra_of
+    in_lane = (order_col == extra_of) & (extra_col > 0.0)
+    tile_row = iota((40, 384), 0).astype(F32)
+    piece_down = iota((256, 1), 0)
+    piece_extra = lax.rem(lax.div(piece_down, 4), 8).astype(F32)
+    piece_head = (lax.div(piece_down, 32) * 4 + lax.rem(piece_down, 4)).astype(F32)
+    in_piece = (order_row == piece_extra) & (extra_row > 0.0)
+    head_lane = iota((256, 32), 1).astype(F32)
+    pick_query, pick_att = [], []
     for m in range(1, 4):
+        mine = jnp.where(here_col & (rank_col == float(m)), 1.0, 0.0)
+        along = jnp.sum(jnp.where(in_lane, mine, 0.0), axis=0, keepdims=True)
+        pick_query.append(jnp.where(tile_row == tile_of, along, 0.0))
         mine = jnp.where(here_row & (rank_row == float(m)), 1.0, 0.0)
-        pick_col.append(jnp.sum(jnp.where(order_is, mine, 0.0), axis=1, keepdims=True))
-        mine = jnp.where(here_col & (rank_col == float(m)), 1.0, 0.0)
-        pick_row.append(jnp.sum(jnp.where(order_at, mine, 0.0), axis=0, keepdims=True))
+        down = jnp.sum(jnp.where(in_piece, mine, 0.0), axis=1, keepdims=True)
+        pick_att.append(jnp.where(head_lane == piece_head, down, 0.0))
+    pick_query = jnp.concatenate(pick_query, axis=0).astype(BF16)
+    pick_att = jnp.concatenate(pick_att, axis=1).astype(BF16)
 
     rows = dot(to_slots, hidden_ref[...])
     squares = jnp.sum(rows * rows, axis=1, keepdims=True)
     scaled = (rows * gain_ref[...].astype(F32)).astype(BF16)
     loads[0].wait()
     loads[1].wait()
+    for load in loads[2:]:
+        load.start()
     for n in range(10):
         weight = wq[:, n * 512 : (n + 1) * 512] if n < 8 else wkv[:, (n - 8) * 512 : (n - 7) * 512]
         part = dot(scaled, weight)
@@ -217,10 +245,10 @@
             j = 4 * n + t
             tile = part[:, t * 128 : (t + 1) * 128]
             blk[pl.ds(j, 64, stride=48), :] = tile[:64]
-            ext[pl.ds(j, 8, stride=40), :] = tile[64:]
-    for e in range(8):
-        for r in range(5):
-            blk[pl.ds(8 * e * 48 + 40 + r, 8, stride=48), :] = ext[pl.ds(e * 40 + r * 8, 8), :]
+            ext[pl.ds(48 * (j // 5) + j % 5, 8, stride=5), :] = tile[64:]
+    for r in range(40, 48):
+        if r != 45:
+            blk[pl.ds(r, 64, stride=48), :] = jnp.zeros((64, 128), F32)
 
     def high_low(value, low):
         high = value.astype(BF16).astype(F32)
@@ -230,10 +258,11 @@
     blk[pl.ds(45, 64, stride=48), :] = high_low(wide[:64], iota((64, 128), 1) >= 64)
     extra_squares = jnp.where(lax.rem(iota((8, 128), 1), 64) == iota((8, 128), 0), wide[64:], 0.0)
     extra_squares = jnp.sum(extra_squares, axis=0, keepdims=True)
-    blk[pl.ds(46, 64, stride=48), :] = jnp.broadcast_to(
-        high_low(extra_squares, lane >= 64), (64, 128)
-    )
-    blk[pl.ds(47, 64, stride=48), :] = jnp.zeros((64, 128), F32)
+    extra_squares = high_low(extra_squares, lane >= 64)
+    for g in range(8):
+        ext[48 * g + 40 : 48 * g + 48, :] = jnp.zeros((8, 128), F32)
+        ext[48 * g + 35 : 48 * g + 36, :] = extra_squares
+        xq_out[g] = ext[48 * g : 48 * g + 48, :].astype(BF16)
 
     def block(slot):
         return blk[pl.ds(pl.multiple_of(slot * 48, 16), 48), :]
@@ -243,29 +272,56 @@
         return carry
 
     lax.fori_loop(0, 32, pack_sibling, 0)
-    pl.semaphore_wait(barrier, 32)
-    exchange = to_sibling(sib_out, sib_in, sib_send.at[0], sib_recv.at[0])
-    exchange.start()
-    exchange.wait()
-
-    def pack(k, carry):
+    pl.semaphore_wait(barrier, 35)
+
+    def ring_start(src, dst, p):
+        def step(i, carry):
+            g, device = ring_member(i)
+            pltpu.make_async_remote_copy(
+                src_ref=src.at[g],
+                dst_ref=dst.at[member],
+                send_sem=ring_send.at[p],
+                recv_sem=ring_recv.at[p],
+                device_id={"pool": device},
+                device_id_type=MESH,
+            ).start()
+            return carry
+
+        lax.fori_loop(1, 8, step, 0)
+        dst[member] = src[member]
+
+    def ring_end(src, dst, p):
+        part7 = pl.ds(0, 7)
+        done = to_sibling(src.at[part7], dst.at[part7], ring_send.at[p], ring_recv.at[p])
+        done.wait()
+        total = dst[0].astype(F32)
+        for g in range(1, 8):
+            total = total + dst[g].astype(F32)
+        return total.astype(BF16)
+
+    ring_start(xq_out, xq_in, 0)
+    exchanges = []
+    for i, a in enumerate(SHIFTS):
+        group = pl.ds(lax.rem(z + a, 4) * 8, 8)
+        exchange = to_sibling(sib_out.at[group], sib_in.at[group], sib_send.at[i], sib_recv.at[i])
+        exchange.start()
+        exchanges.append(exchange)
+
+    def pack(k):
         rs_out[k] = (block(core * 32 + k) + sib_in[k].astype(F32)).astype(BF16)
-        return carry
-
-    lax.fori_loop(0, 32, pack, 0)
-    each_chip(
-        lambda a, c: remote(rs_out.at[c], rs_in.at[chip], rs_send.at[0], rs_recv.at[0], c).start()
-    )
+
+    for i, a in enumerate(SHIFTS):
+        exchanges[i].wait_recv()
+
+        def send_sum(k, carry, a=a):
+            c = target(a, k)
+            pack(c)
+            remote(rs_out.at[c], rs_in.at[chip], rs_send.at[0], rs_recv.at[0], c).start()
+            return carry
+
+        lax.fori_loop(0, 8 if a else 7, send_sum, 0)
+    pack(chip)
     rs_in[chip] = rs_out[chip]
-    part31 = pl.ds(0, 31)
-    done = remote(rs_out.at[part31], rs_in.at[part31], rs_send.at[0], rs_recv.at[0], chip)
-    done.wait_recv()
-
-    def add(k, total):
-        return total + rs_in[k].astype(F32)
-
-    summed = lax.fori_loop(0, 32, add, jnp.zeros((48, 128), F32))
-    done.wait_send()
 
     def gather_start(buf, p):
         each_chip(
@@ -274,40 +330,61 @@
             ).start()
         )
 
+    def gather_forward_one(buf, p, a):
+        some = buf.at[pl.ds(0, 8 if a else 7)]
+        remote(some, some, ag_send.at[p], ag_recv.at[p * 4 + a], chip).wait_recv()
+        group = buf.at[pl.ds(core * 32 + lax.rem(z + 4 - a, 4) * 8, 8)]
+        send = to_sibling(group, group, fwd_send.at[p * 4 + a], fwd_recv.at[p * 4 + a])
+        send.start()
+        return send
+
     def gather_forward(buf, p):
-        sends = []
-        for a in SHIFTS:
-            some = buf.at[pl.ds(0, 8 if a else 7)]
-            remote(some, some, ag_send.at[p], ag_recv.at[p * 4 + a], chip).wait_recv()
-            group = buf.at[pl.ds(core * 32 + lax.rem(z + 4 - a, 4) * 8, 8)]
-            send = to_sibling(group, group, fwd_send.at[p * 4 + a], fwd_recv.at[p * 4 + a])
-            send.start()
-            sends.append(send)
-        return sends
+        return [gather_forward_one(buf, p, a) for a in SHIFTS]
+
+    def gather_drain(buf, p):
+        some = buf.at[pl.ds(0, 31)]
+        remote(some, some, ag_send.at[p], ag_recv.at[p * 4], chip).wait_send()
 
     def gather_end(buf, p, sends):
         for send in sends:
             send.wait()
-        some = buf.at[pl.ds(0, 31)]
-        remote(some, some, ag_send.at[p], ag_recv.at[p * 4], chip).wait_send()
-
-    qe_buf[my_slot] = summed[40:48]
-    gather_start(qe_buf, 0)
-    sends = gather_forward(qe_buf, 0)
-    gather_end(qe_buf, 0, sends)
+        gather_drain(buf, p)
+
+    xq_buf[my_slot] = ring_end(xq_out, xq_in, 0)
+    gather_start(xq_buf, 0)
+    sends = gather_forward(xq_buf, 0)
+    part31 = pl.ds(0, 31)
+    done = remote(rs_out.at[part31], rs_in.at[part31], rs_send.at[0], rs_recv.at[0], chip)
+    done.wait_recv()
+
+    def add(k, total):
+        return total + rs_in[k].astype(F32)
+
+    summed = lax.fori_loop(0, 32, add, jnp.zeros((48, 128), F32))
+    done.wait_send()
+    for exchange in exchanges:
+        exchange.wait_send()
+    gather_end(xq_buf, 0, sends)
+
+    def ring_total(buf, g, shape):
+        first = (g % 2) * 32 + (g // 2) * 2
+
+        def step(k, total):
+            return total + buf[first + k * 8].astype(F32) + buf[first + k * 8 + 1].astype(F32)
+
+        return lax.fori_loop(0, 4, step, jnp.zeros(shape, F32))
 
     own_squares = jnp.sum(summed[45:46], axis=1, keepdims=True) * (1.0 / 64.0)
-    requests = [summed[:40] * lax.rsqrt(own_squares * (1.0 / MODEL) + EPSILON)]
-    for e in range(EXTRA):
-        for r in range(5):
-            piece = qe_buf[pl.ds(8 * e, 8), r, :]
-            qe[e, pl.ds(8 * r, 8), :] = piece
-    for m in range(3):
-        total = jnp.zeros((40, 128), F32)
-        for e in range(EXTRA):
-            total = total + pick_col[m][e : e + 1] * qe[e]
-        sq = jnp.sum(pick_row[m] * summed[46:47], axis=1, keepdims=True)
-        requests.append(total * lax.rsqrt(sq * (1.0 / MODEL) + EPSILON))
+    first = summed[:40] * lax.rsqrt(own_squares * (1.0 / MODEL) + EPSILON)
+    pieces = [ring_total(xq_buf, g, (48, 128)) for g in range(8)]
+    of_extra = lax.rem(iota((48, 128), 1), 64).astype(F32) == floor_div(
+        iota((48, 128), 0).astype(F32), 5
+    )
+    extra_factor = jnp.sum(jnp.where(of_extra, pieces[0][35:36], 0.0), axis=1, keepdims=True)
+    extra_factor = lax.rsqrt(extra_factor * (1.0 / MODEL) + EPSILON)
+    extra_rows = jnp.concatenate([(p * extra_factor).astype(BF16) for p in pieces], axis=0)
+    further = dot(pick_query, extra_rows)
+    requests = [first] + [further[40 * m : 40 * (m + 1)] for m in range(3)]
     query = jnp.concatenate([r[:32] for r in requests], axis=0).astype(BF16).astype(F32)
     new_keys = jnp.concatenate([r[32:36] for r in requests], axis=0).astype(BF16)
     new_values = jnp.concatenate([r[36:40] for r in requests], axis=0).astype(BF16)
@@ -363,83 +440,34 @@
     own_spread = jnp.where(lax.div(iota((128, 16), 0), 8) == iota((128, 16), 1), own_col, 0.0)
     att = (att + dot(own_spread.astype(BF16), new_values)) / total_col
 
-    att_buf[my_slot] = att[:32].astype(BF16)
+    att = att.astype(BF16)
+    pieces = dot(pick_att, att[32:]).astype(BF16)
+    for g in range(8):
+        xa_out[g] = pieces[32 * g : 32 * (g + 1)]
+    ring_start(xa_out, xa_in, 1)
+    att_buf[my_slot] = att[:32]
     gather_start(att_buf, 1)
-    for e in range(EXTRA):
-        piece = jnp.zeros((32, 128), F32)
-        for m in range(3):
-            piece = piece + pick_col[m][e : e + 1] * att[32 * (m + 1) : 32 * (m + 2)]
-        xo_out[2 * e] = piece[:16].astype(BF16)
-        xo_out[2 * e + 1] = piece[16:].astype(BF16)
-    exchange = to_sibling(
-        xo_out.at[pl.ds((1 - core) * 7, 7)], xo_in, sib_send.at[1], sib_recv.at[1]
-    )
-    exchange.start()
-    exchange.wait()
-
-    def reducer(j):
-        return 5 * j + core
-
-    def reduce_send(j, carry):
-        xr_out[j] = (xo_out[core * 7 + j].astype(F32) + xo_in[j].astype(F32)).astype(BF16)
-
-        @pl.when(reducer(j) == chip)
-        def _():
-            xr_in[chip] = xr_out[j]
-
-        @pl.when(reducer(j) != chip)
-        def _():
-            remote(
-                xr_out.at[j], xr_in.at[chip], rs_send.at[1], rs_recv.at[1], reducer(j)
-            ).start()
-
-        return carry
-
-    lax.fori_loop(0, 7, reduce_send, 0)
-    is_reducer = lax.rem(chip + 5 - core, 5) == 0
-    my_chunk = lax.div(chip - core, 5)
-
-    def many(ref, n, send, recv):
-        some = ref.at[pl.ds(0, n)]
-        return remote(some, some, send, recv, chip)
-
-    @pl.when(is_reducer)
-    def _():
-        many(xr_in, 31, rs_send.at[1], rs_recv.at[1]).wait_recv()
-        xa_buf[core * 7 + my_chunk] = lax.fori_loop(
-            0, 32, lambda k, t: t + xr_in[k].astype(F32), jnp.zeros((16, 128), F32)
-        ).astype(BF16)
-        mine = xa_buf.at[core * 7 + my_chunk]
-        each_chip(lambda a, c: remote(mine, mine, rs_send.at[2], rs_recv.at[2], c).start())
-        many(xr_out, 6, rs_send.at[1], rs_recv.at[1]).wait_send()
-        many(xa_buf, 6, rs_send.at[2], rs_recv.at[2]).wait_recv()
-
-    @pl.when(jnp.logical_not(is_reducer))
-    def _():
-        many(xr_out, 7, rs_send.at[1], rs_recv.at[1]).wait_send()
-        many(xa_buf, 7, rs_send.at[2], rs_recv.at[2]).wait_recv()
-
-    half = xa_buf.at[pl.ds(core * 7, 7)]
-    exchange = to_sibling(half, half, sib_send.at[2], sib_recv.at[2])
-    exchange.start()
+    xa_buf[my_slot] = ring_end(xa_out, xa_in, 1)
+    gather_start(xa_buf, 3)
     sends = gather_forward(att_buf, 1)
+    extra_sends = gather_forward(xa_buf, 3)
     gather_end(att_buf, 1, sends)
-    exchange.wait()
-
-    @pl.when(is_reducer)
-    def _():
-        many(xr_in, 31, rs_send.at[2], rs_recv.at[2]).wait_send()
 
     def widen(s, carry):
         spread[pl.ds(pl.multiple_of(s * 32, 32), 32), :] = att_buf[s].astype(F32)
         return carry
 
     lax.fori_loop(0, 64, widen, 0)
-    for q in range(14):
-        spread[pl.ds(2048 + 16 * q, 16), :] = xa_buf[q].astype(F32)
-    spread[pl.ds(2048 + 224, 32), :] = jnp.zeros((32, 128), F32)
+    gather_end(xa_buf, 3, extra_sends)
+    for g in range(8):
+        spread_extra[32 * g : 32 * (g + 1), :] = ring_total(xa_buf, g, (32, 128))
     for h in range(32):
-        lhs[:, h * 128 : (h + 1) * 128] = spread[pl.ds(h, 72, stride=32), :].astype(BF16)
+        at = slice(h * 128, (h + 1) * 128)
+        lhs[:64, at] = spread[pl.ds(h, 64, stride=32), :].astype(BF16)
+        lhs[64:, at] = jnp.concatenate(
+            [spread_extra[pl.ds(32 * (h // 4) + h % 4, 8, stride=4), :], jnp.zeros((8, 128), F32)],
+            axis=0,
+        ).astype(BF16)
     loads[4].wait()
     projected = dot(lhs[...], wout[...])
     moved = jnp.zeros((64, 128), F32)
@@ -451,28 +479,43 @@
 
     res_buf[my_slot] = residual
     gather_start(res_buf, 2)
-    sends = gather_forward(res_buf, 2)
-    gather_end(res_buf, 2, sends)
-
-    def scale_ffn(p, squares):
-        value = res_buf[lax.rem(p, 2) * 32 + lax.div(p, 2)].astype(F32)
-        gain = ffn_gain_ref[pl.ds(p, 1), :]
-        lhs_ffn[:, pl.ds(pl.multiple_of(p * 128, 128), 128)] = (value * gain).astype(BF16)
-        return squares + value * value
-
-    squares = lax.fori_loop(0, 64, scale_ffn, jnp.zeros((64, 128), F32))
-    factor = lax.rsqrt(jnp.sum(squares, axis=1, keepdims=True) * (1.0 / MODEL) + EPSILON)
     loads[5].wait()
     loads[6].wait()
 
-    def hidden_units(i, carry):
-        gate, up = carry
-        at = pl.ds(pl.multiple_of(i * 1024, 1024), 1024)
-        some = lhs_ffn[:, at]
-        return gate + dot(some, wgate[at, :]), up + dot(some, wup[at, :])
+    def hidden_units(a, parity, carry):
+        def step(k, carry):
+            squares, gate, up = carry
+            some, gates, ups = [], [], []
+            for n in range(2):
+                c = lax.rem(z + 4 - a, 4) * 8 + 2 * k + n
+                at = pl.ds(pl.multiple_of((2 * c + parity) * 128, 128), 128)
+                value = res_buf[parity * 32 + c].astype(F32)
+                squares = squares + value * value
+                some.append((value * ffn_gain_ref[:, at].astype(F32)).astype(BF16))
+                gates.append(wgate[at, :])
+                ups.append(wup[at, :])
+            some = jnp.concatenate(some, axis=1)
+            gate = gate + dot(some, jnp.concatenate(gates, axis=0))
+            up = up + dot(some, jnp.concatenate(ups, axis=0))
+            return squares, gate, up
+
+        return lax.fori_loop(0, 4, step, carry)
 
     zero = jnp.zeros((64, 256), F32)
-    gate, up = lax.fori_loop(0, 8, hidden_units, (zero, zero))
+    carry = (jnp.zeros((64, 128), F32), zero, zero)
+    sends = []
+    for i, a in enumerate(SHIFTS):
+        sends.append(gather_forward_one(res_buf, 2, a))
+        carry = hidden_units(a, core, carry)
+        if i:
+            sends[i - 1].wait_recv()
+            carry = hidden_units(SHIFTS[i - 1], 1 - core, carry)
+    sends[3].wait_recv()
+    squares, gate, up = hidden_units(SHIFTS[3], 1 - core, carry)
+    gather_drain(res_buf, 2)
+    for send in sends:
+        send.wait_send()
+    factor = lax.rsqrt(jnp.sum(squares, axis=1, keepdims=True) * (1.0 / MODEL) + EPSILON)
     gate = gate * factor
     inner = (gate / (1.0 + jnp.exp(-gate)) * (up * factor)).astype(BF16)
 
@@ -506,13 +549,13 @@
             n = 8 * i + c - first
             total = stage[16 * i + 2 * (c - first) + core] + dsib_in[n].astype(F32)
             drs_out[n] = total.astype(BF16)
-            remote(drs_out.at[n], drs_in.at[chip], rs_send.at[3], rs_recv.at[3], c).start()
+            remote(drs_out.at[n], drs_in.at[chip], rs_send.at[1], rs_recv.at[1], c).start()
             return carry
 
         lax.fori_loop(0, 8 if a else 7, send_down, 0)
     k = chip - z * 8
     drs_in[chip] = (stage[48 + 2 * k + core] + dsib_in[24 + k].astype(F32)).astype(BF16)
-    done = many(drs_in, 31, rs_send.at[3], rs_recv.at[3])
+    done = remote(drs_out.at[part31], drs_in.at[part31], rs_send.at[1], rs_recv.at[1], chip)
     done.wait_recv()
     shares = lax.fori_loop(
         0, 32, lambda k, t: t + drs_in[k].astype(F32), jnp.zeros((64, 128), F32)
@@ -558,38 +601,39 @@
             V((SLOTS, 512), BF16),
             V((SLOTS, 512), BF16),
             V((64 * 48, 128), F32),
-            V((320, 128), F32),
+            V((8 * 48, 128), F32),
             V((32, 48, 128), BF16),
             V((32, 48, 128), BF16),
             V((32, 48, 128), BF16),
             V((32, 48, 128), BF16),
-            V((64, 8, 128), F32),
-            V((7, 40, 128), F32),
+            V((8, 48, 128), BF16),
+            V((8, 48, 128), BF16),
+            V((64, 48, 128), BF16),
             V((SLOTS, 128), F32),
             V((64, 32, 128), BF16),
-            V((14, 16, 128), BF16),
-            V((7, 16, 128), BF16),
-            V((7, 16, 128), BF16),
-            V((32, 16, 128), BF16),
-            V((14, 16, 128), BF16),
-            V((72 * 32, 128), F32),
-            V((72, 4096), BF16),
+            V((8, 32, 128), BF16),
+            V((8, 32, 128), BF16),
+            V((64, 32, 128), BF16),
+            V((64 * 32, 128), F32),
+            V((256, 128), F32),
+            V((80, 4096), BF16),
             V((64, 64, 128), BF16),
-            V((64, 8192), BF16),
             V((64, 64, 128), F32),
             V((32, 64, 128), BF16),
             V((32, 64, 128), BF16),
             V((32, 64, 128), BF16),
             V((32, 64, 128), BF16),
             dma((8,)),
-            dma((3,)),
-            dma((3,)),
             dma((4,)),
             dma((4,)),
-            dma((3,)),
-            dma((12,)),
-            dma((12,)),
-            dma((12,)),
+            dma((2,)),
+            dma((2,)),
+            dma((2,)),
+            dma((2,)),
+            dma((4,)),
+            dma((16,)),
+            dma((16,)),
+            dma((16,)),
             dma((4,)),
             dma((4,)),
         ],
@@ -599,7 +643,7 @@
     )(
         hidden_in,
         attn_gain.reshape(1, 128),
-        ffn_gain.reshape(64, 128).astype(F32),
+        ffn_gain.reshape(1, 8192),
         lengths.reshape(1, 64),
         home_device.reshape(1, 64),
         offset.reshape(1, 64),

time: 79.8 us -> 73.6 us (0.922)
  Pallas kernels: 76.9 us -> 70.6 us
  local copies, waits for them, and re-layouts: 1.32 us -> 2.66 us
  other arithmetic: 1.32 us -> 0 us
    pallas_call x1, Pallas kernels: 76.9 us -> 70.6 us  [local(): pl.pallas_call(kernel, out_shape=jax.ShapeDtypeStruct((64, 128), BF16), i...]
    reshape x0 -> x1, local copies, waits for them, and re-layouts: none -> 1.34 us  [local(): ffn_gain.reshape(1, 8192)]
    convert_element_type x1 -> x0, other arithmetic: 1.32 us -> none  [local(): ffn_gain.reshape(64, 128).astype(F32)]
where the time goes in v2:
time: 73.6 us; the launch traced here: 73.3 us
  Pallas kernels  70.6 us (96%)
  local copies, waits for them, and re-layouts  2.66 us (4%)
    pallas_call x1, Pallas kernels, local(): pl.pallas_call(kernel, out_shape=jax.ShapeDtypeStruct((64, 128), BF16), i...  70.6 us

profile of v2, /device:TPU:1, one launch (start us, length us, event | category | flops | bytes accessed | tf_op | source)
XLA Modules:
  0.0 73.3 jit_solution(15897206734505721233)
XLA Ops:
  0.0 1.3 %reshape.16.ffn_gain_ref = bf16[1,8192]{1,0:T(2,128)(2,1)} reshape(bf16[8192]{0:T(1024)(128)(2,1)} %param.19) | data formatting | bytes 32768 | tf_op jit(solution)/shard_map/reshape | solution.py:646
  1.3 70.6 %shard_map.136 = bf16[64,128]{1,0:T(8,128)(2,1)} custom-call(bf16[64,128]{1,0:T(8,128)(2,1)} %hidden_ref.1, bf16[1,128]{1,0:T(2,128)(2,1)} %bitcast.4, bf16[1,8192]{1,0:T(2,128)(2,1)} %reshape.16.ffn_gain_ref, s32[1,64]{1,0:T(1,128)} %bitcast.5, s32[1,64]{1,0:T(1,128)} %bitcast.6, s32[1,64]{1,0:T(1,128)} %bitcast.7, bf16[128,4096]{1,0:T(8,128)(2,1)} %wq_hbm.1, ...), custom_call_target="tpu_custom_call" | custom-call | tf_op jit(solution)/shard_map/pallas_call | solution.py:589
  72.0 1.3 %copy.16 = bf16[64,128]{1,0:T(8,128)(2,1)} copy(bf16[64,128]{1,0:T(8,128)(2,1)} %shard_map.136) | data formatting | bytes 32768

commit v3 on v2

--- a/solution.py
+++ b/solution.py
@@ -11,7 +11,8 @@
 EPSILON = 1e-05
 MODEL = 8192
 SLOTS = 5120
-CHUNK = 512
+SCORE = 1024
+MIX = 1024
 SHIFTS = (2, 1, 3, 0)
 EXTRA = 7
 
@@ -25,12 +26,12 @@
 
 
 def kernel(
-    hidden_ref,
-    gain_ref,
-    ffn_gain_ref,
-    lengths_ref,
-    home_ref,
-    offset_ref,
+    hidden_hbm,
+    gain_hbm,
+    ffn_gain_hbm,
+    lengths_hbm,
+    home_hbm,
+    offset_hbm,
     wq_hbm,
     wkv_hbm,
     wout_hbm,
@@ -40,6 +41,13 @@
     keys_hbm,
     values_hbm,
     out_ref,
+    hidden_ref,
+    gain_ref,
+    ffn_gain_ref,
+    lengths_ref,
+    home_ref,
+    offset_ref,
+    gain_rows,
     wq,
     wkv,
     wout,
@@ -72,6 +80,7 @@
     drs_out,
     drs_in,
     load_sem,
+    small_sem,
     sib_send,
     sib_recv,
     ring_send,
@@ -160,8 +169,25 @@
             ]
         )
     ]
-    loads[0].start()
-    loads[1].start()
+    small = [
+        pltpu.make_async_copy(src, dst, small_sem.at[i])
+        for i, (src, dst) in enumerate(
+            [
+                (home_hbm, home_ref),
+                (hidden_hbm, hidden_ref),
+                (gain_hbm, gain_ref),
+                (offset_hbm, offset_ref),
+                (lengths_hbm, lengths_ref),
+                (ffn_gain_hbm, ffn_gain_ref),
+            ]
+        )
+    ]
+    for load in small + loads[:2]:
+        load.start()
+    for load in small:
+        load.wait()
+
+    gain_rows[...] = ffn_gain_ref[...].reshape(64, 128).astype(F32)
 
     home_row = jnp.broadcast_to(home_ref[...].astype(F32), (64, 64))
     down_i = iota((64, 64), 0)
@@ -404,29 +430,33 @@
     loads[2].wait()
 
     def score(i, best):
-        at = pl.ds(pl.multiple_of(i * CHUNK, CHUNK), CHUNK)
+        at = pl.ds(pl.multiple_of(i * SCORE, SCORE), SCORE)
         s = dot(keys[at, :], spread_query) * scale
-        slot = iota((CHUNK, 128), 0) + i * CHUNK
+        slot = iota((SCORE, 128), 0) + i * SCORE
         s = jnp.where((slot >= start) & (slot < stop), s, -jnp.inf)
         scores[at, :] = s
-        return jnp.maximum(best, jnp.max(s.reshape(CHUNK // 8, 8, 128), axis=0))
-
-    best = lax.fori_loop(0, SLOTS // CHUNK, score, jnp.full((8, 128), -jnp.inf, F32))
+        return jnp.maximum(best, jnp.max(s.reshape(SCORE // 8, 8, 128), axis=0))
+
+    best = lax.fori_loop(0, SLOTS // SCORE, score, jnp.full((8, 128), -jnp.inf, F32), unroll=True)
     top = jnp.maximum(jnp.max(best, axis=0, keepdims=True), own)
     loads[3].wait()
 
     def mix(i, carry):
         total, mixed = carry
-        at = pl.ds(pl.multiple_of(i * CHUNK, CHUNK), CHUNK)
+        at = pl.ds(pl.multiple_of(i * MIX, MIX), MIX)
         w = jnp.exp(scores[at, :] - top)
-        total = total + jnp.sum(w.reshape(CHUNK // 8, 8, 128), axis=0)
+        total = total + jnp.sum(w.reshape(MIX // 8, 8, 128), axis=0)
         mixed = mixed + lax.dot_general(
             w.astype(BF16), values[at, :], (((0,), (0,)), ((), ())), preferred_element_type=F32
         )
         return total, mixed
 
     total, mixed = lax.fori_loop(
-        0, SLOTS // CHUNK, mix, (jnp.zeros((8, 128), F32), jnp.zeros((128, 512), F32))
+        0,
+        SLOTS // MIX,
+        mix,
+        (jnp.zeros((8, 128), F32), jnp.zeros((128, 512), F32)),
+        unroll=True,
     )
     own_weight = jnp.exp(own - top)
     total = jnp.sum(total, axis=0, keepdims=True) + own_weight
@@ -491,7 +521,7 @@
                 at = pl.ds(pl.multiple_of((2 * c + parity) * 128, 128), 128)
                 value = res_buf[parity * 32 + c].astype(F32)
                 squares = squares + value * value
-                some.append((value * ffn_gain_ref[:, at].astype(F32)).astype(BF16))
+                some.append((value * gain_rows[pl.ds(2 * c + parity, 1), :]).astype(BF16))
                 gates.append(wgate[at, :])
                 ups.append(wup[at, :])
             some = jnp.concatenate(some, axis=1)
@@ -499,7 +529,7 @@
             up = up + dot(some, jnp.concatenate(ups, axis=0))
             return squares, gate, up
 
-        return lax.fori_loop(0, 4, step, carry)
+        return lax.fori_loop(0, 4, step, carry, unroll=True)
 
     zero = jnp.zeros((64, 256), F32)
     carry = (jnp.zeros((64, 128), F32), zero, zero)
@@ -589,9 +619,16 @@
     return pl.pallas_call(
         kernel,
         out_shape=jax.ShapeDtypeStruct((64, 128), BF16),
-        in_specs=[vmem] * 6 + [hbm] * 8,
+        in_specs=[hbm] * 14,
         out_specs=vmem,
         scratch_shapes=[
+            V((64, 128), BF16),
+            V((1, 128), BF16),
+            V((8192,), BF16),
+            V((1, 64), jnp.int32),
+            V((1, 64), jnp.int32),
+            V((1, 64), jnp.int32),
+            V((64, 128), F32),
             V((128, 4096), BF16),
             V((128, 1024), BF16),
             V((4096, 128), BF16),
@@ -624,6 +661,7 @@
             V((32, 64, 128), BF16),
             V((32, 64, 128), BF16),
             dma((8,)),
+            dma((6,)),
             dma((4,)),
             dma((4,)),
             dma((2,)),
@@ -643,7 +681,7 @@
     )(
         hidden_in,
         attn_gain.reshape(1, 128),
-        ffn_gain.reshape(1, 8192),
+        ffn_gain,
         lengths.reshape(1, 64),
         home_device.reshape(1, 64),
         offset.reshape(1, 64),

time: 73.6 us -> 66.7 us (0.906)
  Pallas kernels: 70.6 us -> 65.2 us
  local copies, waits for them, and re-layouts: 2.66 us -> 1.32 us
    pallas_call x1, Pallas kernels: 70.6 us -> 65.2 us  [local(): pl.pallas_call(kernel, out_shape=jax.ShapeDtypeStruct((64, 128), BF16), i...]
    reshape x1 -> x0, local copies, waits for them, and re-layouts: 1.34 us -> none  [local(): ffn_gain.reshape(1, 8192)]
where the time goes in v3:
time: 66.7 us; the launch traced here: 66.5 us
  Pallas kernels  65.2 us (98%)
  local copies, waits for them, and re-layouts  1.32 us (2%)
    pallas_call x1, Pallas kernels, local(): pl.pallas_call(kernel, out_shape=jax.ShapeDtypeStruct((64, 128), BF16), i...  65.2 us

profile of v3, /device:TPU:1, one launch (start us, length us, event | category | flops | bytes accessed | tf_op | source)
XLA Modules:
  0.0 66.5 jit_solution(9453805990232663190)
XLA Ops:
  0.0 65.2 %shard_map.136 = bf16[64,128]{1,0:T(8,128)(2,1)} custom-call(bf16[64,128]{1,0:T(8,128)(2,1)} %hidden_hbm.1, bf16[1,128]{1,0:T(2,128)(2,1)} %bitcast.4, bf16[8192]{0:T(1024)(128)(2,1)} %ffn_gain_hbm.1, s32[1,64]{1,0:T(1,128)} %bitcast.5, s32[1,64]{1,0:T(1,128)} %bitcast.6, s32[1,64]{1,0:T(1,128)} %bitcast.7, bf16[128,4096]{1,0:T(8,128)(2,1)} %wq_hbm.1, ...), custom_call_target="tpu_custom_call" | custom-call | tf_op jit(solution)/shard_map/pallas_call | solution.py:619
  65.2 1.3 %copy.16 = bf16[64,128]{1,0:T(8,128)(2,1)} copy(bf16[64,128]{1,0:T(8,128)(2,1)} %shard_map.136) | data formatting | bytes 32768

commit v4 on v3

--- a/solution.py
+++ b/solution.py
@@ -297,7 +297,7 @@
         sib_out[k] = block((1 - core) * 32 + k).astype(BF16)
         return carry
 
-    lax.fori_loop(0, 32, pack_sibling, 0)
+    lax.fori_loop(0, 32, pack_sibling, 0, unroll=8)
     pl.semaphore_wait(barrier, 35)
 
     def ring_start(src, dst, p):
@@ -386,7 +386,7 @@
     def add(k, total):
         return total + rs_in[k].astype(F32)
 
-    summed = lax.fori_loop(0, 32, add, jnp.zeros((48, 128), F32))
+    summed = lax.fori_loop(0, 32, add, jnp.zeros((48, 128), F32), unroll=16)
     done.wait_send()
     for exchange in exchanges:
         exchange.wait_send()
@@ -398,7 +398,7 @@
         def step(k, total):
             return total + buf[first + k * 8].astype(F32) + buf[first + k * 8 + 1].astype(F32)
 
-        return lax.fori_loop(0, 4, step, jnp.zeros(shape, F32))
+        return lax.fori_loop(0, 4, step, jnp.zeros(shape, F32), unroll=True)
 
     own_squares = jnp.sum(summed[45:46], axis=1, keepdims=True) * (1.0 / 64.0)
     first = summed[:40] * lax.rsqrt(own_squares * (1.0 / MODEL) + EPSILON)
@@ -487,7 +487,7 @@
         spread[pl.ds(pl.multiple_of(s * 32, 32), 32), :] = att_buf[s].astype(F32)
         return carry
 
-    lax.fori_loop(0, 64, widen, 0)
+    lax.fori_loop(0, 64, widen, 0, unroll=16)
     gather_end(xa_buf, 3, extra_sends)
     for g in range(8):
         spread_extra[32 * g : 32 * (g + 1), :] = ring_total(xa_buf, g, (32, 128))
@@ -563,7 +563,7 @@
             dsib_out[8 * i + k] = stage[16 * i + 2 * k + 1 - core].astype(BF16)
             return carry
 
-        lax.fori_loop(0, 8, pack_down, 0)
+        lax.fori_loop(0, 8, pack_down, 0, unroll=True)
         group = pl.ds(8 * i, 8)
         exchange = to_sibling(
             dsib_out.at[group], dsib_in.at[group], dsib_send.at[i], dsib_recv.at[i]
@@ -588,7 +588,7 @@
     done = remote(drs_out.at[part31], drs_in.at[part31], rs_send.at[1], rs_recv.at[1], chip)
     done.wait_recv()
     shares = lax.fori_loop(
-        0, 32, lambda k, t: t + drs_in[k].astype(F32), jnp.zeros((64, 128), F32)
+        0, 32, lambda k, t: t + drs_in[k].astype(F32), jnp.zeros((64, 128), F32), unroll=16
     )
     out_ref[...] = (residual.astype(F32) + shares).astype(BF16)
     done.wait_send()

time: 66.7 us -> 65.8 us (0.987)
  Pallas kernels: 65.2 us -> 64.3 us
    pallas_call x1, Pallas kernels: 65.2 us -> 64.3 us  [local(): pl.pallas_call(kernel, out_shape=jax.ShapeDtypeStruct((64, 128), BF16), i...]
where the time goes in v4:
time: 65.8 us; the launch traced here: 65.6 us
  Pallas kernels  64.3 us (98%)
  local copies, waits for them, and re-layouts  1.32 us (2%)
    pallas_call x1, Pallas kernels, local(): pl.pallas_call(kernel, out_shape=jax.ShapeDtypeStruct((64, 128), BF16), i...  64.3 us
    unnamed x1, local copies, waits for them, and re-layouts  1.32 us

profile of v4, /device:TPU:1, one launch (start us, length us, event | category | flops | bytes accessed | tf_op | source)
XLA Modules:
  0.0 65.6 jit_solution(956954525895709008)
XLA Ops:
  0.0 64.3 %shard_map.136 = bf16[64,128]{1,0:T(8,128)(2,1)} custom-call(bf16[64,128]{1,0:T(8,128)(2,1)} %hidden_hbm.1, bf16[1,128]{1,0:T(2,128)(2,1)} %bitcast.4, bf16[8192]{0:T(1024)(128)(2,1)} %ffn_gain_hbm.1, s32[1,64]{1,0:T(1,128)} %bitcast.5, s32[1,64]{1,0:T(1,128)} %bitcast.6, s32[1,64]{1,0:T(1,128)} %bitcast.7, bf16[128,4096]{1,0:T(8,128)(2,1)} %wq_hbm.1, ...), custom_call_target="tpu_custom_call" | custom-call | tf_op jit(solution)/shard_map/pallas_call | solution.py:619
  64.3 1.3 %copy.16 = bf16[64,128]{1,0:T(8,128)(2,1)} copy(bf16[64,128]{1,0:T(8,128)(2,1)} %shard_map.136) | data formatting | bytes 32768

commit v5 on v4

--- a/solution.py
+++ b/solution.py
@@ -137,10 +137,15 @@
             device_id_type=MESH,
         )
 
-    member = x * 2 + core
-
-    def ring_member(i):
-        g = lax.rem(member + i, 8)
+    plane_member = lax.div(chip, 2) * 2 + core
+    ring_of = x * 2 + core
+
+    def plane(i):
+        g = lax.rem(plane_member + i, 32)
+        return g, (lax.div(g, 2) * 2 + y) * 2 + lax.rem(g, 2)
+
+    def ring(i):
+        g = lax.rem(ring_of + i, 8)
         return g, (z * 8 + lax.div(g, 2) * 2 + y) * 2 + lax.rem(g, 2)
 
     barrier = pltpu.get_barrier_semaphore()
@@ -150,9 +155,13 @@
         )
     )
     pl.semaphore_signal(barrier, inc=1, device_id={"pool": sibling}, device_id_type=MESH)
-    for i in range(1, 4):
-        other = (z * 8 + lax.rem(x + i, 4) * 2 + y) * 2 + 1 - core
+
+    def greet_plane(i, carry):
+        other = (lax.rem(lax.div(chip, 2) + i, 16) * 2 + y) * 2 + 1 - core
         pl.semaphore_signal(barrier, inc=1, device_id={"pool": other}, device_id_type=MESH)
+        return carry
+
+    lax.fori_loop(1, 16, greet_plane, 0)
 
     loads = [
         pltpu.make_async_copy(src, dst, load_sem.at[i])
@@ -234,22 +243,26 @@
     def floor_div(value, n):
         return jnp.floor((value + 0.5) * (1.0 / n))
 
-    chunk_lane = iota((1, 384), 1).astype(F32)
-    chunk_of = floor_div(chunk_lane, 48)
-    chunk_row = chunk_lane - 48.0 * chunk_of
-    extra_of = floor_div(chunk_row, 5)
-    tile_of = 5.0 * chunk_of + chunk_row - 5.0 * extra_of
-    in_lane = (order_col == extra_of) & (extra_col > 0.0)
-    tile_row = iota((40, 384), 0).astype(F32)
+    chunk_lane = iota((1, 512), 1)
+    chunk_row = lax.rem(chunk_lane, 16).astype(F32)
+    flat = lax.div(chunk_lane, 16).astype(F32) * 9.0 + chunk_row
+    extra_of = floor_div(flat, 40)
+    tile_of = flat - 40.0 * extra_of
+    in_lane = (order_col == extra_of) & (extra_col > 0.0) & (chunk_row < 9.0)
+    in_squares = (order_col == lax.rem(iota((64, 128), 1), 64).astype(F32)) & (extra_col > 0.0)
+    tile_row = iota((40, 512), 0).astype(F32)
     piece_down = iota((256, 1), 0)
     piece_extra = lax.rem(lax.div(piece_down, 4), 8).astype(F32)
     piece_head = (lax.div(piece_down, 32) * 4 + lax.rem(piece_down, 4)).astype(F32)
     in_piece = (order_row == piece_extra) & (extra_row > 0.0)
     head_lane = iota((256, 32), 1).astype(F32)
-    pick_query, pick_att = [], []
+    pick_query, pick_att, pick_squares = [], [], []
     for m in range(1, 4):
         mine = jnp.where(here_col & (rank_col == float(m)), 1.0, 0.0)
         along = jnp.sum(jnp.where(in_lane, mine, 0.0), axis=0, keepdims=True)
+        pick_squares.append(
+            jnp.sum(jnp.where(in_squares, mine, 0.0), axis=0, keepdims=True)
+        )
         pick_query.append(jnp.where(tile_row == tile_of, along, 0.0))
         mine = jnp.where(here_row & (rank_row == float(m)), 1.0, 0.0)
         down = jnp.sum(jnp.where(in_piece, mine, 0.0), axis=1, keepdims=True)
@@ -271,7 +284,7 @@
             j = 4 * n + t
             tile = part[:, t * 128 : (t + 1) * 128]
             blk[pl.ds(j, 64, stride=48), :] = tile[:64]
-            ext[pl.ds(48 * (j // 5) + j % 5, 8, stride=5), :] = tile[64:]
+            ext[pl.ds(j, 8, stride=40), :] = tile[64:]
     for r in range(40, 48):
         if r != 45:
             blk[pl.ds(r, 64, stride=48), :] = jnp.zeros((64, 128), F32)
@@ -285,10 +298,9 @@
     extra_squares = jnp.where(lax.rem(iota((8, 128), 1), 64) == iota((8, 128), 0), wide[64:], 0.0)
     extra_squares = jnp.sum(extra_squares, axis=0, keepdims=True)
     extra_squares = high_low(extra_squares, lane >= 64)
-    for g in range(8):
-        ext[48 * g + 40 : 48 * g + 48, :] = jnp.zeros((8, 128), F32)
-        ext[48 * g + 35 : 48 * g + 36, :] = extra_squares
-        xq_out[g] = ext[48 * g : 48 * g + 48, :].astype(BF16)
+    for g in range(32):
+        piece = jnp.where(iota((16, 128), 0) == 9, extra_squares, ext[9 * g : 9 * g + 16, :])
+        xq_out[g] = piece.astype(BF16)
 
     def block(slot):
         return blk[pl.ds(pl.multiple_of(slot * 48, 16), 48), :]
@@ -298,11 +310,11 @@
         return carry
 
     lax.fori_loop(0, 32, pack_sibling, 0, unroll=8)
-    pl.semaphore_wait(barrier, 35)
-
-    def ring_start(src, dst, p):
+    pl.semaphore_wait(barrier, 47)
+
+    def ring_start(src, dst, p, member, partner, n):
         def step(i, carry):
-            g, device = ring_member(i)
+            g, device = partner(i)
             pltpu.make_async_remote_copy(
                 src_ref=src.at[g],
                 dst_ref=dst.at[member],
@@ -313,19 +325,19 @@
             ).start()
             return carry
 
-        lax.fori_loop(1, 8, step, 0)
+        lax.fori_loop(1, n, step, 0)
         dst[member] = src[member]
 
-    def ring_end(src, dst, p):
-        part7 = pl.ds(0, 7)
-        done = to_sibling(src.at[part7], dst.at[part7], ring_send.at[p], ring_recv.at[p])
+    def ring_end(src, dst, p, n):
+        rest = pl.ds(0, n - 1)
+        done = to_sibling(src.at[rest], dst.at[rest], ring_send.at[p], ring_recv.at[p])
         done.wait()
         total = dst[0].astype(F32)
-        for g in range(1, 8):
+        for g in range(1, n):
             total = total + dst[g].astype(F32)
         return total.astype(BF16)
 
-    ring_start(xq_out, xq_in, 0)
+    ring_start(xq_out, xq_in, 0, plane_member, plane, 32)
     exchanges = []
     for i, a in enumerate(SHIFTS):
         group = pl.ds(lax.rem(z + a, 4) * 8, 8)
@@ -376,7 +388,7 @@
             send.wait()
         gather_drain(buf, p)
 
-    xq_buf[my_slot] = ring_end(xq_out, xq_in, 0)
+    xq_buf[my_slot] = ring_end(xq_out, xq_in, 0, 32)
     gather_start(xq_buf, 0)
     sends = gather_forward(xq_buf, 0)
     part31 = pl.ds(0, 31)
@@ -402,15 +414,19 @@
 
     own_squares = jnp.sum(summed[45:46], axis=1, keepdims=True) * (1.0 / 64.0)
     first = summed[:40] * lax.rsqrt(own_squares * (1.0 / MODEL) + EPSILON)
-    pieces = [ring_total(xq_buf, g, (48, 128)) for g in range(8)]
-    of_extra = lax.rem(iota((48, 128), 1), 64).astype(F32) == floor_div(
-        iota((48, 128), 0).astype(F32), 5
-    )
-    extra_factor = jnp.sum(jnp.where(of_extra, pieces[0][35:36], 0.0), axis=1, keepdims=True)
-    extra_factor = lax.rsqrt(extra_factor * (1.0 / MODEL) + EPSILON)
-    extra_rows = jnp.concatenate([(p * extra_factor).astype(BF16) for p in pieces], axis=0)
-    further = dot(pick_query, extra_rows)
-    requests = [first] + [further[40 * m : 40 * (m + 1)] for m in range(3)]
+    pieces = []
+    for g in range(32):
+        slot = (g % 2) * 32 + (g // 2) * 2
+        pieces.append(xq_buf[slot].astype(F32) + xq_buf[slot + 1].astype(F32))
+    extra_squares = pieces[0][9:10]
+    rows = jnp.concatenate(pieces, axis=0)
+    high = rows.astype(BF16)
+    further = dot(pick_query, high) + dot(pick_query, (rows - high.astype(F32)).astype(BF16))
+    factors = [
+        lax.rsqrt(jnp.sum(p * extra_squares, axis=1, keepdims=True) * (1.0 / MODEL) + EPSILON)
+        for p in pick_squares
+    ]
+    requests = [first] + [further[40 * m : 40 * (m + 1)] * factors[m] for m in range(3)]
     query = jnp.concatenate([r[:32] for r in requests], axis=0).astype(BF16).astype(F32)
     new_keys = jnp.concatenate([r[32:36] for r in requests], axis=0).astype(BF16)
     new_values = jnp.concatenate([r[36:40] for r in requests], axis=0).astype(BF16)
@@ -474,10 +490,10 @@
     pieces = dot(pick_att, att[32:]).astype(BF16)
     for g in range(8):
         xa_out[g] = pieces[32 * g : 32 * (g + 1)]
-    ring_start(xa_out, xa_in, 1)
+    ring_start(xa_out, xa_in, 1, ring_of, ring, 8)
     att_buf[my_slot] = att[:32]
     gather_start(att_buf, 1)
-    xa_buf[my_slot] = ring_end(xa_out, xa_in, 1)
+    xa_buf[my_slot] = ring_end(xa_out, xa_in, 1, 8)
     gather_start(xa_buf, 3)
     sends = gather_forward(att_buf, 1)
     extra_sends = gather_forward(xa_buf, 3)
@@ -638,14 +654,14 @@
             V((SLOTS, 512), BF16),
             V((SLOTS, 512), BF16),
             V((64 * 48, 128), F32),
-            V((8 * 48, 128), F32),
+            V((320, 128), F32),
             V((32, 48, 128), BF16),
             V((32, 48, 128), BF16),
             V((32, 48, 128), BF16),
             V((32, 48, 128), BF16),
-            V((8, 48, 128), BF16),
-            V((8, 48, 128), BF16),
-            V((64, 48, 128), BF16),
+            V((32, 16, 128), BF16),
+            V((32, 16, 128), BF16),
+            V((64, 16, 128), BF16),
             V((SLOTS, 128), F32),
             V((64, 32, 128), BF16),
             V((8, 32, 128), BF16),

time: 65.8 us -> 64.2 us (0.976)
  Pallas kernels: 64.3 us -> 62.6 us
    pallas_call x1, Pallas kernels: 64.3 us -> 62.6 us  [local(): pl.pallas_call(kernel, out_shape=jax.ShapeDtypeStruct((64, 128), BF16), i...]
where the time goes in v5:
time: 64.2 us; the launch traced here: 64 us
  Pallas kernels  62.6 us (98%)
  local copies, waits for them, and re-layouts  1.32 us (2%)
    pallas_call x1, Pallas kernels, local(): pl.pallas_call(kernel, out_shape=jax.ShapeDtypeStruct((64, 128), BF16), i...  62.6 us
    unnamed x1, local copies, waits for them, and re-layouts  1.32 us

profile of v5, /device:TPU:1, one launch (start us, length us, event | category | flops | bytes accessed | tf_op | source)
XLA Modules:
  0.0 64.0 jit_solution(14012931719639837513)
XLA Ops:
  0.0 62.6 %shard_map.136 = bf16[64,128]{1,0:T(8,128)(2,1)} custom-call(bf16[64,128]{1,0:T(8,128)(2,1)} %hidden_hbm.1, bf16[1,128]{1,0:T(2,128)(2,1)} %bitcast.4, bf16[8192]{0:T(1024)(128)(2,1)} %ffn_gain_hbm.1, s32[1,64]{1,0:T(1,128)} %bitcast.5, s32[1,64]{1,0:T(1,128)} %bitcast.6, s32[1,64]{1,0:T(1,128)} %bitcast.7, bf16[128,4096]{1,0:T(8,128)(2,1)} %wq_hbm.1, ...), custom_call_target="tpu_custom_call" | custom-call | tf_op jit(solution)/shard_map/pallas_call | solution.py:635
  62.6 1.3 %copy.16 = bf16[64,128]{1,0:T(8,128)(2,1)} copy(bf16[64,128]{1,0:T(8,128)(2,1)} %shard_map.136) | data formatting | bytes 32768

commit v6 on v5

--- a/solution.py
+++ b/solution.py
@@ -357,7 +357,7 @@
             remote(rs_out.at[c], rs_in.at[chip], rs_send.at[0], rs_recv.at[0], c).start()
             return carry
 
-        lax.fori_loop(0, 8 if a else 7, send_sum, 0)
+        lax.fori_loop(0, 8 if a else 7, send_sum, 0, unroll=True)
     pack(chip)
     rs_in[chip] = rs_out[chip]
 
@@ -595,18 +595,23 @@
             n = 8 * i + c - first
             total = stage[16 * i + 2 * (c - first) + core] + dsib_in[n].astype(F32)
             drs_out[n] = total.astype(BF16)
-            remote(drs_out.at[n], drs_in.at[chip], rs_send.at[1], rs_recv.at[1], c).start()
+            remote(drs_out.at[n], drs_in.at[chip], rs_send.at[1], rs_recv.at[2 + a], c).start()
             return carry
 
-        lax.fori_loop(0, 8 if a else 7, send_down, 0)
+        lax.fori_loop(0, 8 if a else 7, send_down, 0, unroll=True)
     k = chip - z * 8
     drs_in[chip] = (stage[48 + 2 * k + core] + dsib_in[24 + k].astype(F32)).astype(BF16)
     done = remote(drs_out.at[part31], drs_in.at[part31], rs_send.at[1], rs_recv.at[1], chip)
-    done.wait_recv()
-    shares = lax.fori_loop(
-        0, 32, lambda k, t: t + drs_in[k].astype(F32), jnp.zeros((64, 128), F32), unroll=16
-    )
-    out_ref[...] = (residual.astype(F32) + shares).astype(BF16)
+    shares = residual.astype(F32)
+    for a in SHIFTS:
+        some = pl.ds(0, 8 if a else 7)
+        remote(
+            drs_out.at[some], drs_in.at[some], rs_send.at[1], rs_recv.at[2 + a], chip
+        ).wait_recv()
+        first = lax.rem(z + 4 - a, 4) * 8
+        for k in range(8):
+            shares = shares + drs_in[first + k].astype(F32)
+    out_ref[...] = shares.astype(BF16)
     done.wait_send()
     for exchange in exchanges:
         exchange.wait_send()
@@ -683,7 +688,7 @@
             dma((2,)),
             dma((2,)),
             dma((2,)),
-            dma((2,)),
+            dma((6,)),
             dma((4,)),
             dma((16,)),
             dma((16,)),

time: 64.2 us -> 64.1 us (level)
  no operation moved by 1% of the time
where the time goes in v6:
time: 64.1 us; the launch traced here: 63.9 us
  Pallas kernels  62.6 us (98%)
  local copies, waits for them, and re-layouts  1.32 us (2%)
    pallas_call x1, Pallas kernels, local(): pl.pallas_call(kernel, out_shape=jax.ShapeDtypeStruct((64, 128), BF16), i...  62.6 us
    unnamed x1, local copies, waits for them, and re-layouts  1.32 us

profile of v6, /device:TPU:1, one launch (start us, length us, event | category | flops | bytes accessed | tf_op | source)
XLA Modules:
  0.0 63.9 jit_solution(15210377176958871606)
XLA Ops:
  0.0 62.6 %shard_map.136 = bf16[64,128]{1,0:T(8,128)(2,1)} custom-call(bf16[64,128]{1,0:T(8,128)(2,1)} %hidden_hbm.1, bf16[1,128]{1,0:T(2,128)(2,1)} %bitcast.4, bf16[8192]{0:T(1024)(128)(2,1)} %ffn_gain_hbm.1, s32[1,64]{1,0:T(1,128)} %bitcast.5, s32[1,64]{1,0:T(1,128)} %bitcast.6, s32[1,64]{1,0:T(1,128)} %bitcast.7, bf16[128,4096]{1,0:T(8,128)(2,1)} %wq_hbm.1, ...), custom_call_target="tpu_custom_call" | custom-call | tf_op jit(solution)/shard_map/pallas_call | solution.py:640
  62.6 1.3 %copy.16 = bf16[64,128]{1,0:T(8,128)(2,1)} copy(bf16[64,128]{1,0:T(8,128)(2,1)} %shard_map.136) | data formatting | bytes 32768
